TPU v7x, 256 devices: a whole 4x4x8 slice. The times are simulated.
256 devices in a mesh: gz: 2 (over x_hi), row: 16 (over z, core), col: 8 (over x_lo, y).
Axes of the slice: x: 4 (x_hi: 2, x_lo: 2; x = x_hi * 2 + x_lo), y: 4, z: 8, core: 2. Of those that a mesh axis runs over, the one named last changes fastest.
Arguments:
- volume: bfloat16 [32, 1024, 2048], P('gz', 'row', 'col'), may hold values from -7 to 7
Outputs:
- tensor: float32 [6, 8, 256, 512], P(None, 'gz', 'row', 'col')
All inputs are finite; a program needn't handle non-finite values.
Results may differ from a plain program's by a relative error of at most 0.0028.
Values may be sent and summed in bfloat16 or wider, within the bound.
A program may use at most 128 MiB of HBM per device.

v0:
```python
import itertools

import jax
import jax.numpy as jnp
import ml_dtypes
import numpy as np
from jax import lax
from jax.experimental import pallas as pl
from jax.experimental.pallas import tpu as pltpu
from jax.sharding import PartitionSpec as P

R = 3
R2 = 8
MARGIN = R + R2
BF16 = ml_dtypes.bfloat16
F32 = jnp.float32
MESH = pl.DeviceIdType.MESH

DZ, DY, DX = 16, 64, 256
WY, GY = DY + 32, DY + 2 * R2
QZ, QY, QX = DZ // 4, DY // 4, DX // 4
SLOT = 16
HALF = DZ // 2
NEIGHBOURS = tuple(o for o in itertools.product((0, 1), (-1, 0, 1), (-1, 0, 1)) if o != (0, 0, 0))
pair_table = ((0, 0), (1, 1), (2, 2), (0, 1), (0, 2), (1, 2))


def gauss_taps(radius):
    offsets = np.arange(-radius, radius + 1).astype(np.float32)
    spread = np.float32(radius / 3.0)
    smooth = np.exp(-offsets * offsets / (np.float32(2.0) * spread * spread))
    smooth = smooth / np.sum(smooth)
    slopes = offsets * smooth
    slopes = slopes / np.sum(offsets * slopes)
    return [t.astype(BF16).astype(np.float32) for t in (smooth, slopes)]


SMOOTH, SLOPE = gauss_taps(R)
WIDE, _ = gauss_taps(R2)


def banded(taps, radius, source, target):
    s = np.asarray(source)[:, None] - np.asarray(target)[None, :]
    picked = taps[np.clip(s + radius, 0, 2 * radius)]
    return np.where(np.abs(s) <= radius, picked, np.float32(0.0))


def layer_targets(gz):
    return [0, 4, 8, 12] + ([16, 20] if gz == 0 else [-8, -4])


def constants():
    y_in, y_out, y_coarse = np.arange(WY) - 16, np.arange(GY) - R2, 4 * np.arange(QY)
    x_all, x_coarse = np.arange(DX), 4 * np.arange(QX)
    ty = []
    for edge in range(3):
        inside = np.ones(GY, np.float32)
        if edge == 0:
            inside[y_out < 0] = 0
        if edge == 2:
            inside[y_out >= DY] = 0
        ty.append(np.concatenate([banded(t, R, y_in, y_out).T * inside[:, None] for t in (SMOOTH, SLOPE)]))
    x_pair = np.stack([banded(SLOPE, R, x_all, x_all), banded(SMOOTH, R, x_all, x_all)])
    ay = banded(WIDE, R2, y_out, y_coarse).T
    near, far = [], []
    for gz in range(2):
        targets = layer_targets(gz)
        near_z, far_z = HALF * (1 - gz) + np.arange(HALF), HALF * gz + np.arange(HALF)
        near.append(np.kron(banded(WIDE, R2, near_z, targets).T, ay))
        far.append(np.kron(banded(WIDE, R2, far_z, targets[:QZ]).T, ay))
    mx = np.zeros((DX, 128), np.float32)
    mx[:, :QX] = banded(WIDE, R2, x_all, x_coarse)
    mx[:R] = 0
    mx[DX - R :] = 0
    cols = np.arange(MARGIN)
    pad_in, pad_out = ((0, SLOT - MARGIN), (0, SLOT - MARGIN)), ((0, 0), (0, 0))
    wp = []
    for side_in, x_out, outside in (
        ((cols - MARGIN, cols), cols - R2, lambda x: x < 0),
        ((cols + DX - MARGIN, cols + DX), cols + DX - R, lambda x: x >= DX),
    ):
        for masked in (False, True):
            blocks = []
            for x_in in side_in:
                row = []
                for t in (SMOOTH, SLOPE):
                    w = banded(t, R, x_in, x_out)
                    if masked:
                        w = np.where(outside(x_out)[None, :], np.float32(0.0), w)
                    row.append(np.kron(np.eye(8, dtype=np.float32), np.pad(w, pad_in)))
                blocks.append(np.concatenate(row, axis=1))
            wp.append(np.concatenate(blocks, axis=0))
    wz, wzx = [], []
    one = np.eye(SLOT, dtype=np.float32)
    for gz in range(2):
        z_halo = DZ + np.arange(8) if gz == 0 else np.arange(8) - R
        rows = []
        for z_in, used in ((np.arange(DZ), DZ), (z_halo, R)):
            keep = (np.arange(len(z_in)) < used)[:, None]
            rows.append(
                np.concatenate(
                    [np.kron(banded(t, R, z_in, np.arange(DZ)) * keep, one) for t in (SMOOTH, SLOPE)], axis=1
                )
            )
        wz.append(np.concatenate(rows, axis=0))
        bz = banded(WIDE, R2, np.arange(DZ), layer_targets(gz))
        sides = []
        for x_out in (cols - R2, cols + DX - R):
            bx = np.zeros((SLOT, 128), np.float32)
            bx[:MARGIN, :QX] = banded(WIDE, R2, x_out, x_coarse)
            sides.append(np.kron(bz, bx))
        wzx.append(np.concatenate(sides, axis=0))
    stacks = (np.stack(ty), x_pair, np.stack(near), np.stack(far), mx, np.stack(wp), np.stack(wz), ay, np.stack(wzx))
    return [np.asarray(a, np.float32).astype(BF16) for a in stacks]


def mm(a, b):
    return jnp.dot(a, b, preferred_element_type=F32)


def kernel(
    n_row, n_col,
    vol, ty_h, xp_h, near_h, far_h, mx_h, wp_h, wz_h, ay_h, wzx_h,
    out,
    f, strips, strips_z, send_z, zs, zd, planes, grads, prods, acc, panel, xpanel, zpanel, gpanel, psend, precv,
    ty, xp, near, far, mx, wpl, wpr, wz, ay, wzx,
    local_sem, send_sem, recv_sem,
):
    gz, row, col = lax.axis_index("gz"), lax.axis_index("row"), lax.axis_index("col")
    has = {(1, -1): row > 0, (1, 1): row < n_row - 1, (2, -1): col > 0, (2, 1): col < n_col - 1}

    def exists(o):
        tests = [has[d, o[d]] for d in (1, 2) if o[d]]
        if not tests:
            return None
        return tests[0] if len(tests) == 1 else tests[0] & tests[1]

    def when(o, fn):
        ok = exists(o)
        if ok is None:
            fn()
        else:
            pl.when(ok)(fn)

    def peer(o):
        return (lax.rem(gz + o[0], 2), row + o[1], col + o[2])

    barrier = pltpu.get_barrier_semaphore()
    count = 0
    for o in NEIGHBOURS:
        when(o, lambda o=o: pl.semaphore_signal(barrier, inc=1, device_id=peer(o), device_id_type=MESH))
        ok = exists(o)
        count = count + (1 if ok is None else ok.astype(jnp.int32))

    own_z, own_y = pl.ds(R, DZ), pl.ds(16, DY)
    first_y, last_y, top_y, bottom_y = pl.ds(16, 16), pl.ds(DY, 16), pl.ds(0, 16), pl.ds(DY + 16, 16)
    load = pltpu.make_async_copy(vol, f.at[own_z, own_y], local_sem.at[0])
    load.start()
    edge = jnp.where(row == 0, 0, jnp.where(row == n_row - 1, 2, 1))
    fetches = [
        (ty_h.at[edge], ty), (xp_h, xp), (near_h.at[gz], near), (far_h.at[gz], far), (mx_h, mx),
        (wp_h.at[(col == 0).astype(jnp.int32)], wpl), (wp_h.at[2 + (col == n_col - 1).astype(jnp.int32)], wpr),
        (wz_h.at[gz], wz), (ay_h, ay), (wzx_h.at[gz], wzx),
    ]
    fetches = [pltpu.make_async_copy(s, d, local_sem.at[1 + i]) for i, (s, d) in enumerate(fetches)]
    for c in fetches:
        c.start()

    dead_z = pl.ds((R + DZ) * gz, R)
    f[dead_z] = jnp.zeros((R, WY, DX), jnp.bfloat16)
    for d, where_y in ((-1, top_y), (1, bottom_y)):
        @pl.when(jnp.logical_not(has[1, d]))
        def _(where_y=where_y):
            f[:, where_y] = jnp.zeros((DZ + 2 * R, 16, DX), jnp.bfloat16)
            strips[:, where_y] = jnp.zeros((4, 16, 256), jnp.bfloat16)
            strips_z[:, where_y] = jnp.zeros((4, 16, 128), jnp.bfloat16)
    for d, kind in ((-1, 0), (1, 3)):
        @pl.when(jnp.logical_not(has[2, d]))
        def _(kind=kind):
            strips[kind] = jnp.zeros((WY, 256), jnp.bfloat16)
            strips_z[kind] = jnp.zeros((WY, 128), jnp.bfloat16)

    load.wait()
    near_z = 13 * (1 - gz)

    def pack(layers):
        lane = lax.broadcasted_iota(jnp.int32, (DY, 128), 1)
        first, last = (jnp.zeros((DY, 128), F32) for _ in range(2))
        for t, z in enumerate(layers):
            tile = f[R + z, 16 : 16 + DY, :]
            use = (lane >= SLOT * t) & (lane < SLOT * t + MARGIN)
            first = jnp.where(use, pltpu.roll(tile[:, :128].astype(F32), SLOT * t, 1), first)
            last = jnp.where(use, pltpu.roll(tile[:, 128:].astype(F32), (SLOT * t + MARGIN) % 128, 1), last)
        return first.astype(jnp.bfloat16), last.astype(jnp.bfloat16)

    for h in range(2):
        first, last = pack([HALF * h + t for t in range(8)])
        strips[1, 16 : 16 + DY, 128 * h : 128 * h + 128] = first
        strips[2, 16 : 16 + DY, 128 * h : 128 * h + 128] = last
    first, last = pack([near_z + t for t in range(R)])
    send_z[0] = first
    send_z[1] = last

    messages = []

    def message(o, source, target):
        i = len(messages)
        c = pltpu.make_async_remote_copy(
            src_ref=source, dst_ref=target, send_sem=send_sem.at[i], recv_sem=recv_sem.at[i],
            device_id=peer(o), device_id_type=MESH,
        )
        messages.append((o, c))

    near_layers, halo_layers = pl.ds(near_z, R), pl.ds((R + DZ) * gz, R)
    both = pl.ds(0, 2)
    own_kinds = pl.ds(1, 2)
    y_cut = {0: (pl.ds(0, DY), own_y), 1: (pl.ds(DY - 16, 16), top_y), -1: (pl.ds(0, 16), bottom_y)}
    for o in sorted(NEIGHBOURS, key=lambda o: -(2 * o[0] + abs(o[1]) + abs(o[2])) - 9 * (o == (1, 0, 0))):
        a, b, c = o
        src_y, dst_y = y_cut[b]
        strip_y = pl.ds(16 + (DY - 16 if b == 1 else 0), DY if b == 0 else 16)
        if c == 0 and a == 0:
            message(o, vol.at[:, src_y], f.at[own_z, dst_y])
            message(o, strips.at[own_kinds, strip_y], strips.at[own_kinds, dst_y])
        elif c == 0:
            message(o, vol.at[near_layers, src_y], f.at[halo_layers, dst_y])
            message(o, send_z.at[both, src_y], strips_z.at[own_kinds, dst_y])
        else:
            mine, theirs = (2, 0) if c == 1 else (1, 3)
            if a == 0:
                message(o, strips.at[mine, strip_y], strips.at[theirs, dst_y])
            else:
                message(o, send_z.at[mine - 1, src_y], strips_z.at[theirs, dst_y])

    pl.semaphore_wait(barrier, count)
    for o, c in messages:
        when(o, lambda c=c: c.start())
    for c in fetches:
        c.wait()
    for o, c in messages:
        when((o[0], -o[1], -o[2]), lambda c=c: c.wait_recv())

    def products(get, put):
        g = [get(i) for i in range(3)]
        for c, (i, j) in enumerate(pair_table):
            put(c, g[i] * g[j])

    for side, (k, w) in enumerate(((0, wpl), (2, wpr))):
        for t in range(3):
            src = [(strips[i, :, 128 * t : 128 * t + 128] if t < 2 else strips_z[i]) for i in (k, k + 1)]
            xs = mm(jnp.concatenate(src, axis=1), w[...]).astype(jnp.bfloat16)
            xpanel[0, :, 128 * t : 128 * t + 128] = xs[:, :128]
            xpanel[1, :, 128 * t : 128 * t + 128] = xs[:, 128:]
        zpanel[0] = mm(xpanel[1], wz[:, :256]).astype(jnp.bfloat16)
        zpanel[1] = mm(xpanel[0], wz[:, :256]).astype(jnp.bfloat16)
        zpanel[2] = mm(xpanel[0], wz[:, 256:]).astype(jnp.bfloat16)
        edge_grads = [
            mm(ty[:GY] if i != 1 else ty[GY:], zpanel[i]).astype(jnp.bfloat16) for i in range(3)
        ]

        def put(c, p, side=side):
            gpanel[16 * c : 16 * c + 16, 256 * side : 256 * side + 256] = mm(ay[...], p).astype(jnp.bfloat16)

        products(lambda i: edge_grads[i], put)
    panel[...] = mm(gpanel[...], wzx[...])

    def gradients(z_base):
        def four_layers(g, _):
            z0 = z_base + 4 * g
            for y in range(0, WY, 16):
                for x in range(0, DX, 128):
                    v = [f[z0 + i, y : y + 16, x : x + 128].astype(F32) for i in range(4 + 2 * R)]
                    for j in range(4):
                        c = v[j : j + 7]
                        smooth, slope = c[3] * float(SMOOTH[R]), None
                        for s in (1, 2, 3):
                            smooth = smooth + (c[3 - s] + c[3 + s]) * float(SMOOTH[R + s])
                            term = (c[3 + s] - c[3 - s]) * float(SLOPE[R + s])
                            slope = term if slope is None else slope + term
                        zs[j, y : y + 16, x : x + 128] = smooth.astype(jnp.bfloat16)
                        zd[j, y : y + 16, x : x + 128] = slope.astype(jnp.bfloat16)
            for j in range(4):
                pair = mm(ty[...], zs[j]).astype(jnp.bfloat16)
                at = slice(GY * j, GY * j + GY)
                planes[0, at] = pair[:GY]
                planes[1, at] = pair[GY:]
                planes[2, at] = mm(ty[:GY], zd[j]).astype(jnp.bfloat16)
            for i in range(3):
                grads[i] = mm(planes[i], xp[0 if i == 0 else 1]).astype(jnp.bfloat16)
            for y in range(0, 4 * GY, 16):
                at = pl.ds(pl.multiple_of(4 * GY * g, 16) + y, 16)

                def put(c, p, at=at):
                    prods[c, at] = p

                products(lambda i, y=y: grads[i, y : y + 16], put)
            return 0

        lax.fori_loop(0, 2, four_layers, 0)

    gradients(HALF * (1 - gz))
    for c in range(6):
        s = mm(near[...], prods[c])
        acc[c] = s[: QZ * QY]
        reach = mm(s[QZ * QY :].astype(jnp.bfloat16), mx[...])
        for q in range(2):
            edge_part = panel[16 * c : 16 * c + 16, 128 * (QZ + q) : 128 * (QZ + q) + 128]
            psend[c, 16 * q : 16 * q + 16] = (reach[16 * q : 16 * q + 16] + edge_part).astype(jnp.bfloat16)
    message((1, 0, 0), psend, precv)
    messages[-1][1].start()

    gradients(HALF * gz)
    for c in range(6):
        s = acc[c] + mm(far[...], prods[c])
        own = mm(s.astype(jnp.bfloat16), mx[...])
        for q in range(QZ):
            part = own[16 * q : 16 * q + 16] + panel[16 * c : 16 * c + 16, 128 * q : 128 * q + 128]
            out[c, q] = part[:, :QX]
    messages[-1][1].wait_recv()
    for q in range(2):
        for c in range(6):
            got = precv[c, 16 * q : 16 * q + 16, :QX].astype(F32)
            out[c, 2 * (1 - gz) + q] += got
    for o, c in messages:
        when(o, lambda c=c: c.wait_send())


def solution(mesh):
    n_row, n_col = mesh.shape["row"], mesh.shape["col"]
    consts = constants()
    bf = jnp.bfloat16
    hbm = pl.BlockSpec(memory_space=pltpu.HBM)

    def per_device(volume):
        return pl.pallas_call(
            lambda *refs: kernel(n_row, n_col, *refs),
            name="structure_tensor",
            out_shape=jax.ShapeDtypeStruct((6, QZ, QY, QX), F32),
            in_specs=[hbm] * (1 + len(consts)),
            out_specs=pl.BlockSpec(memory_space=pltpu.VMEM),
            scratch_shapes=[
                pltpu.VMEM((DZ + 2 * R, WY, DX), bf),
                pltpu.VMEM((4, WY, 256), bf),
                pltpu.VMEM((4, WY, 128), bf),
                pltpu.VMEM((2, DY, 128), bf),
                pltpu.VMEM((4, WY, DX), bf),
                pltpu.VMEM((4, WY, DX), bf),
                pltpu.VMEM((3, 4 * GY, DX), bf),
                pltpu.VMEM((3, 4 * GY, DX), bf),
                pltpu.VMEM((6, HALF * GY, DX), bf),
                pltpu.VMEM((6, QZ * QY, DX), F32),
                pltpu.VMEM((96, 768), F32),
                pltpu.VMEM((2, WY, 384), bf),
                pltpu.VMEM((3, WY, 256), bf),
                pltpu.VMEM((96, 512), bf),
                pltpu.VMEM((6, 32, 128), bf),
                pltpu.VMEM((6, 32, 128), bf),
                pltpu.VMEM((2 * GY, WY), bf),
                pltpu.VMEM((2, DX, DX), bf),
                pltpu.VMEM((6 * 16, HALF * GY), bf),
                pltpu.VMEM((4 * 16, HALF * GY), bf),
                pltpu.VMEM((DX, 128), bf),
                pltpu.VMEM((256, 256), bf),
                pltpu.VMEM((256, 256), bf),
                pltpu.VMEM((384, 512), bf),
                pltpu.VMEM((16, GY), bf),
                pltpu.VMEM((512, 768), bf),
                pltpu.SemaphoreType.DMA((11,)),
                pltpu.SemaphoreType.DMA((23,)),
                pltpu.SemaphoreType.DMA((23,)),
            ],
            compiler_params=pltpu.CompilerParams(
                collective_id=0, has_side_effects=True, vmem_limit_bytes=32 * 2**20
            ),
        )(volume, *[jnp.asarray(a) for a in consts])

    return jax.shard_map(
        per_device,
        mesh=mesh,
        in_specs=(P("gz", "row", "col"),),
        out_specs=P(None, "gz", "row", "col"),
        check_vma=False,
    )
```

profile of v0, /device:TPU:1, one launch (start us, length us, event | category | flops | bytes accessed | tf_op | source)
XLA Modules:
  0.0 32.6 jit_solution(6310719738878363944)
XLA Ops:
  0.0 0.0 copy-start
  0.0 1.4 %copy-done = bf16[2,512,768]{2,1,0:T(8,128)(2,1)S(1)} copy-done((bf16[2,512,768]{2,1,0:T(8,128)(2,1)S(1)}, bf16[2,512,768]{2,1,0:T(8,128)(2,1)}, u32[]{:S(2)}) %copy-start) | copy-done | bytes 1572888
  1.4 0.0 copy-start.1
  1.4 1.1 %copy-done.1 = bf16[2,384,512]{2,1,0:T(8,128)(2,1)S(1)} copy-done((bf16[2,384,512]{2,1,0:T(8,128)(2,1)S(1)}, bf16[2,384,512]{2,1,0:T(8,128)(2,1)}, u32[]{:S(2)}) %copy-start.1) | copy-done | bytes 786456
  2.5 0.0 copy-start.2
  2.5 1.0 %copy-done.2 = bf16[16,64,256]{2,1,0:T(8,128)(2,1)S(1)} copy-done((bf16[16,64,256]{2,1,0:T(8,128)(2,1)S(1)}, bf16[16,64,256]{2,1,0:T(8,128)(2,1)}, u32[]{:S(2)}) %copy-start.2) | copy-done | bytes 524312
  3.6 0.0 copy-start.3
  3.6 1.0 %copy-done.3 = bf16[4,256,256]{2,1,0:T(8,128)(2,1)S(1)} copy-done((bf16[4,256,256]{2,1,0:T(8,128)(2,1)S(1)}, bf16[4,256,256]{2,1,0:T(8,128)(2,1)}, u32[]{:S(2)}) %copy-start.3) | copy-done | bytes 524312
  4.6 0.0 copy-start.4
  4.6 0.9 %copy-done.4 = bf16[2,256,256]{2,1,0:T(8,128)(2,1)S(1)} copy-done((bf16[2,256,256]{2,1,0:T(8,128)(2,1)S(1)}, bf16[2,256,256]{2,1,0:T(8,128)(2,1)}, u32[]{:S(2)}) %copy-start.4) | copy-done | bytes 262168
  5.6 0.0 copy-start.5
  5.6 0.9 %copy-done.5 = bf16[2,96,640]{2,1,0:T(8,128)(2,1)S(1)} copy-done((bf16[2,96,640]{2,1,0:T(8,128)(2,1)S(1)}, bf16[2,96,640]{2,1,0:T(8,128)(2,1)}, u32[]{:S(2)}) %copy-start.5) | copy-done | bytes 245784
  6.5 0.0 copy-start.6
  6.5 0.9 %copy-done.6 = bf16[2,64,640]{2,1,0:T(8,128)(2,1)S(1)} copy-done((bf16[2,64,640]{2,1,0:T(8,128)(2,1)S(1)}, bf16[2,64,640]{2,1,0:T(8,128)(2,1)}, u32[]{:S(2)}) %copy-start.6) | copy-done | bytes 163864
  7.4 0.0 copy-start.7
  7.4 0.9 %copy-done.7 = bf16[3,160,96]{2,1,0:T(8,128)(2,1)S(1)} copy-done((bf16[3,160,96]{2,1,0:T(8,128)(2,1)S(1)}, bf16[3,160,96]{2,1,0:T(8,128)(2,1)}, u32[]{:S(2)}) %copy-start.7) | copy-done | bytes 92184
  8.3 0.0 copy-start.8
  8.3 0.8 %copy-done.8 = bf16[256,128]{1,0:T(8,128)(2,1)S(1)} copy-done((bf16[256,128]{1,0:T(8,128)(2,1)S(1)}, bf16[256,128]{1,0:T(8,128)(2,1)}, u32[]{:S(2)}) %copy-start.8) | copy-done | bytes 65560
  9.2 0.0 copy-start.9
  9.2 0.7 %copy-done.9 = bf16[16,80]{1,0:T(8,128)(2,1)S(1)} copy-done((bf16[16,80]{1,0:T(8,128)(2,1)S(1)}, bf16[16,80]{1,0:T(8,128)(2,1)}, u32[]{:S(2)}) %copy-start.9) | copy-done | bytes 2584
  9.9 22.0 %structure_tensor.1 = f32[6,4,16,64]{3,2,1,0:T(8,128)S(1)} custom-call(bf16[16,64,256]{2,1,0:T(8,128)(2,1)S(1)} %copy-done.2, bf16[3,160,96]{2,1,0:T(8,128)(2,1)S(1)} %copy-done.7, bf16[2,256,256]{2,1,0:T(8,128)(2,1)S(1)} %copy-done.4, bf16[2,96,640]{2,1,0:T(8,128)(2,1)S(1)} %copy-done.5, bf16[2,64,640]{2,1,0:T(8,128)(2,1)S(1)} %copy-done.6, ...), custom_call_target="tpu_custom_call" | custom-call | tf_op jit(solution)/shard_map/structure_tensor/pallas_call | solution.py:335
  31.9 0.7 %copy.12 = f32[6,4,16,64]{3,2,1,0:T(8,128)} copy(f32[6,4,16,64]{3,2,1,0:T(8,128)S(1)} %structure_tensor.1) | data formatting | bytes 196608
Async XLA Ops:
  0.0 1.4 %copy-start = (bf16[2,512,768]{2,1,0:T(8,128)(2,1)S(1)}, bf16[2,512,768]{2,1,0:T(8,128)(2,1)}, u32[]{:S(2)}) copy-start(bf16[2,512,768]{2,1,0:T(8,128)(2,1)} %constant.26.clone.refs_9_) | copy-start | bytes 4718596
  1.4 1.1 %copy-start.1 = (bf16[2,384,512]{2,1,0:T(8,128)(2,1)S(1)}, bf16[2,384,512]{2,1,0:T(8,128)(2,1)}, u32[]{:S(2)}) copy-start(bf16[2,384,512]{2,1,0:T(8,128)(2,1)} %constant.24.clone.refs_7_) | copy-start | bytes 2359300
  2.5 1.0 %copy-start.2 = (bf16[16,64,256]{2,1,0:T(8,128)(2,1)S(1)}, bf16[16,64,256]{2,1,0:T(8,128)(2,1)}, u32[]{:S(2)}) copy-start(bf16[16,64,256]{2,1,0:T(8,128)(2,1)} %refs_0_.1) | copy-start | bytes 1572868
  3.6 1.0 %copy-start.3 = (bf16[4,256,256]{2,1,0:T(8,128)(2,1)S(1)}, bf16[4,256,256]{2,1,0:T(8,128)(2,1)}, u32[]{:S(2)}) copy-start(bf16[4,256,256]{2,1,0:T(8,128)(2,1)} %constant.23.clone.refs_6_) | copy-start | bytes 1572868
  4.6 0.9 %copy-start.4 = (bf16[2,256,256]{2,1,0:T(8,128)(2,1)S(1)}, bf16[2,256,256]{2,1,0:T(8,128)(2,1)}, u32[]{:S(2)}) copy-start(bf16[2,256,256]{2,1,0:T(8,128)(2,1)} %constant.19.clone.refs_2_) | copy-start | bytes 786436
  5.6 0.9 %copy-start.5 = (bf16[2,96,640]{2,1,0:T(8,128)(2,1)S(1)}, bf16[2,96,640]{2,1,0:T(8,128)(2,1)}, u32[]{:S(2)}) copy-start(bf16[2,96,640]{2,1,0:T(8,128)(2,1)} %constant.20.clone.refs_3_) | copy-start | bytes 737284
  6.5 0.9 %copy-start.6 = (bf16[2,64,640]{2,1,0:T(8,128)(2,1)S(1)}, bf16[2,64,640]{2,1,0:T(8,128)(2,1)}, u32[]{:S(2)}) copy-start(bf16[2,64,640]{2,1,0:T(8,128)(2,1)} %constant.21.clone.refs_4_) | copy-start | bytes 491524
  7.4 0.9 %copy-start.7 = (bf16[3,160,96]{2,1,0:T(8,128)(2,1)S(1)}, bf16[3,160,96]{2,1,0:T(8,128)(2,1)}, u32[]{:S(2)}) copy-start(bf16[3,160,96]{2,1,0:T(8,128)(2,1)} %constant.18.clone.refs_1_) | copy-start | bytes 276484
  8.3 0.8 %copy-start.8 = (bf16[256,128]{1,0:T(8,128)(2,1)S(1)}, bf16[256,128]{1,0:T(8,128)(2,1)}, u32[]{:S(2)}) copy-start(bf16[256,128]{1,0:T(8,128)(2,1)} %constant.22.clone.refs_5_) | copy-start | bytes 196612
  9.2 0.7 %copy-start.9 = (bf16[16,80]{1,0:T(8,128)(2,1)S(1)}, bf16[16,80]{1,0:T(8,128)(2,1)}, u32[]{:S(2)}) copy-start(bf16[16,80]{1,0:T(8,128)(2,1)} %constant.25.clone.refs_8_) | copy-start | bytes 7684
where the time goes:
time: 33 us; the launch traced here: 32.6 us
  Pallas kernels  22 us (67%)
  local copies, waits for them, and re-layouts  10.5 us (32%)
    pallas_call x1, Pallas kernels, per_device(): pl.pallas_call(lambda *refs: kernel(n_row, n_col, *refs), name='structure...  22 us
    unnamed x21, local copies, waits for them, and re-layouts  10.5 us

commit v1 on v0

--- a/solution.py
+++ b/solution.py
@@ -21,6 +21,7 @@
 QZ, QY, QX = DZ // 4, DY // 4, DX // 4
 SLOT = 16
 HALF = DZ // 2
+VMEM_BYTES = 32 * 2**20
 NEIGHBOURS = tuple(o for o in itertools.product((0, 1), (-1, 0, 1), (-1, 0, 1)) if o != (0, 0, 0))
 pair_table = ((0, 0), (1, 1), (2, 2), (0, 1), (0, 2), (1, 2))
 
@@ -110,8 +111,21 @@
             bx[:MARGIN, :QX] = banded(WIDE, R2, x_out, x_coarse)
             sides.append(np.kron(bz, bx))
         wzx.append(np.concatenate(sides, axis=0))
-    stacks = (np.stack(ty), x_pair, np.stack(near), np.stack(far), mx, np.stack(wp), np.stack(wz), ay, np.stack(wzx))
-    return [np.asarray(a, np.float32).astype(BF16) for a in stacks]
+    named = {"ty": ty, "xp": [x_pair.reshape(2 * DX, DX)], "near": near, "far": far, "mx": [mx], "wp": wp, "wz": wz, "ay": [ay], "wzx": wzx}
+    return pack_table(named)
+
+
+def pack_table(named):
+    blocks, places, at = [], {}, 0
+    for name, variants in named.items():
+        rows, lanes = variants[0].shape
+        cuts = -(-lanes // 256)
+        places[name] = (at, rows, cuts)
+        for m in variants:
+            wide = np.pad(np.asarray(m, np.float32), ((0, 0), (0, 256 * cuts - lanes)))
+            blocks += [wide[:, 256 * i : 256 * i + 256] for i in range(cuts)]
+            at += rows * cuts
+    return np.concatenate(blocks, axis=0).astype(BF16), places
 
 
 def mm(a, b):
@@ -119,8 +133,8 @@
 
 
 def kernel(
-    n_row, n_col,
-    vol, ty_h, xp_h, near_h, far_h, mx_h, wp_h, wz_h, ay_h, wzx_h,
+    n_row, n_col, places,
+    vol, table,
     out,
     f, strips, strips_z, send_z, zs, zd, planes, grads, prods, acc, panel, xpanel, zpanel, gpanel, psend, precv,
     ty, xp, near, far, mx, wpl, wpr, wz, ay, wzx,
@@ -157,12 +171,20 @@
     load = pltpu.make_async_copy(vol, f.at[own_z, own_y], local_sem.at[0])
     load.start()
     edge = jnp.where(row == 0, 0, jnp.where(row == n_row - 1, 2, 1))
-    fetches = [
-        (ty_h.at[edge], ty), (xp_h, xp), (near_h.at[gz], near), (far_h.at[gz], far), (mx_h, mx),
-        (wp_h.at[(col == 0).astype(jnp.int32)], wpl), (wp_h.at[2 + (col == n_col - 1).astype(jnp.int32)], wpr),
-        (wz_h.at[gz], wz), (ay_h, ay), (wzx_h.at[gz], wzx),
-    ]
-    fetches = [pltpu.make_async_copy(s, d, local_sem.at[1 + i]) for i, (s, d) in enumerate(fetches)]
+    fetches = []
+    for name, variant, target in (
+        ("ty", edge, ty), ("xp", 0, xp), ("near", gz, near), ("far", gz, far), ("mx", 0, mx),
+        ("wp", (col == 0).astype(jnp.int32), wpl), ("wp", 2 + (col == n_col - 1).astype(jnp.int32), wpr),
+        ("wz", gz, wz), ("ay", 0, ay), ("wzx", gz, wzx),
+    ):
+        base, rows, cuts = places[name]
+        for i in range(cuts):
+            start = pl.multiple_of(base + rows * (cuts * variant + i), 16)
+            fetches.append(
+                pltpu.make_async_copy(
+                    table.at[pl.ds(start, rows)], target.at[:, pl.ds(256 * i, 256)], local_sem.at[1 + len(fetches)]
+                )
+            )
     for c in fetches:
         c.start()
 
@@ -255,11 +277,11 @@
         zpanel[1] = mm(xpanel[0], wz[:, :256]).astype(jnp.bfloat16)
         zpanel[2] = mm(xpanel[0], wz[:, 256:]).astype(jnp.bfloat16)
         edge_grads = [
-            mm(ty[:GY] if i != 1 else ty[GY:], zpanel[i]).astype(jnp.bfloat16) for i in range(3)
+            mm(ty[:GY, :WY] if i != 1 else ty[GY:, :WY], zpanel[i]).astype(jnp.bfloat16) for i in range(3)
         ]
 
         def put(c, p, side=side):
-            gpanel[16 * c : 16 * c + 16, 256 * side : 256 * side + 256] = mm(ay[...], p).astype(jnp.bfloat16)
+            gpanel[16 * c : 16 * c + 16, 256 * side : 256 * side + 256] = mm(ay[:, :GY], p).astype(jnp.bfloat16)
 
         products(lambda i: edge_grads[i], put)
     panel[...] = mm(gpanel[...], wzx[...])
@@ -280,13 +302,13 @@
                         zs[j, y : y + 16, x : x + 128] = smooth.astype(jnp.bfloat16)
                         zd[j, y : y + 16, x : x + 128] = slope.astype(jnp.bfloat16)
             for j in range(4):
-                pair = mm(ty[...], zs[j]).astype(jnp.bfloat16)
+                pair = mm(ty[:, :WY], zs[j]).astype(jnp.bfloat16)
                 at = slice(GY * j, GY * j + GY)
                 planes[0, at] = pair[:GY]
                 planes[1, at] = pair[GY:]
-                planes[2, at] = mm(ty[:GY], zd[j]).astype(jnp.bfloat16)
+                planes[2, at] = mm(ty[:GY, :WY], zd[j]).astype(jnp.bfloat16)
             for i in range(3):
-                grads[i] = mm(planes[i], xp[0 if i == 0 else 1]).astype(jnp.bfloat16)
+                grads[i] = mm(planes[i], xp[:DX] if i == 0 else xp[DX:]).astype(jnp.bfloat16)
             for y in range(0, 4 * GY, 16):
                 at = pl.ds(pl.multiple_of(4 * GY * g, 16) + y, 16)
 
@@ -300,9 +322,9 @@
 
     gradients(HALF * (1 - gz))
     for c in range(6):
-        s = mm(near[...], prods[c])
+        s = mm(near[:, : HALF * GY], prods[c])
         acc[c] = s[: QZ * QY]
-        reach = mm(s[QZ * QY :].astype(jnp.bfloat16), mx[...])
+        reach = mm(s[QZ * QY :].astype(jnp.bfloat16), mx[:, :128])
         for q in range(2):
             edge_part = panel[16 * c : 16 * c + 16, 128 * (QZ + q) : 128 * (QZ + q) + 128]
             psend[c, 16 * q : 16 * q + 16] = (reach[16 * q : 16 * q + 16] + edge_part).astype(jnp.bfloat16)
@@ -311,8 +333,8 @@
 
     gradients(HALF * gz)
     for c in range(6):
-        s = acc[c] + mm(far[...], prods[c])
-        own = mm(s.astype(jnp.bfloat16), mx[...])
+        s = acc[c] + mm(far[:, : HALF * GY], prods[c])
+        own = mm(s.astype(jnp.bfloat16), mx[:, :128])
         for q in range(QZ):
             part = own[16 * q : 16 * q + 16] + panel[16 * c : 16 * c + 16, 128 * q : 128 * q + 128]
             out[c, q] = part[:, :QX]
@@ -327,16 +349,16 @@
 
 def solution(mesh):
     n_row, n_col = mesh.shape["row"], mesh.shape["col"]
-    consts = constants()
+    table, places = constants()
     bf = jnp.bfloat16
     hbm = pl.BlockSpec(memory_space=pltpu.HBM)
 
     def per_device(volume):
         return pl.pallas_call(
-            lambda *refs: kernel(n_row, n_col, *refs),
+            lambda *refs: kernel(n_row, n_col, places, *refs),
             name="structure_tensor",
             out_shape=jax.ShapeDtypeStruct((6, QZ, QY, QX), F32),
-            in_specs=[hbm] * (1 + len(consts)),
+            in_specs=[hbm, hbm],
             out_specs=pl.BlockSpec(memory_space=pltpu.VMEM),
             scratch_shapes=[
                 pltpu.VMEM((DZ + 2 * R, WY, DX), bf),
@@ -355,24 +377,24 @@
                 pltpu.VMEM((96, 512), bf),
                 pltpu.VMEM((6, 32, 128), bf),
                 pltpu.VMEM((6, 32, 128), bf),
-                pltpu.VMEM((2 * GY, WY), bf),
-                pltpu.VMEM((2, DX, DX), bf),
-                pltpu.VMEM((6 * 16, HALF * GY), bf),
-                pltpu.VMEM((4 * 16, HALF * GY), bf),
-                pltpu.VMEM((DX, 128), bf),
+                pltpu.VMEM((2 * GY, 256), bf),
+                pltpu.VMEM((2 * DX, DX), bf),
+                pltpu.VMEM((6 * 16, 768), bf),
+                pltpu.VMEM((4 * 16, 768), bf),
+                pltpu.VMEM((DX, 256), bf),
                 pltpu.VMEM((256, 256), bf),
                 pltpu.VMEM((256, 256), bf),
                 pltpu.VMEM((384, 512), bf),
-                pltpu.VMEM((16, GY), bf),
+                pltpu.VMEM((16, 256), bf),
                 pltpu.VMEM((512, 768), bf),
-                pltpu.SemaphoreType.DMA((11,)),
+                pltpu.SemaphoreType.DMA((20,)),
                 pltpu.SemaphoreType.DMA((23,)),
                 pltpu.SemaphoreType.DMA((23,)),
             ],
             compiler_params=pltpu.CompilerParams(
-                collective_id=0, has_side_effects=True, vmem_limit_bytes=32 * 2**20
+                collective_id=0, has_side_effects=True, vmem_limit_bytes=VMEM_BYTES
             ),
-        )(volume, *[jnp.asarray(a) for a in consts])
+        )(*[pltpu.with_memory_space_constraint(a, pltpu.HBM) for a in (volume, jnp.asarray(table))])
 
     return jax.shard_map(
         per_device,

time: 33 us -> 23.1 us (0.70); the launches traced: 32.6 us -> 23 us
  local copies, waits for them, and re-layouts: 10.5 us -> 0.68 us
    unnamed x21 -> x1, local copies, waits for them, and re-layouts: 10.5 us -> 0.68 us
where the time goes in v1:
time: 23.1 us; the launch traced here: 23 us
  Pallas kernels  22.3 us (97%)
  local copies, waits for them, and re-layouts  0.68 us (3%)
    pallas_call x1, Pallas kernels, per_device(): pl.pallas_call(lambda *refs: kernel(n_row, n_col, places, *refs), name='s...  22.3 us
    unnamed x1, local copies, waits for them, and re-layouts  0.68 us

profile of v1, /device:TPU:1, one launch (start us, length us, event | category | flops | bytes accessed | tf_op | source)
XLA Modules:
  0.0 23.0 jit_solution(5341538848768484245)
XLA Ops:
  0.0 22.3 %structure_tensor.1 = f32[6,4,16,64]{3,2,1,0:T(8,128)S(1)} custom-call(bf16[16,64,256]{2,1,0:T(8,128)(2,1)} %refs_0_.1, bf16[7856,256]{1,0:T(8,128)(2,1)} %constant.2.clone.refs_1_), custom_call_target="tpu_custom_call" | custom-call | tf_op jit(solution)/shard_map/structure_tensor/pallas_call | solution.py:357
  22.3 0.7 %copy.4 = f32[6,4,16,64]{3,2,1,0:T(8,128)} copy(f32[6,4,16,64]{3,2,1,0:T(8,128)S(1)} %structure_tensor.1) | data formatting | bytes 196608

commit v2 on v1

--- a/solution.py
+++ b/solution.py
@@ -21,6 +21,7 @@
 QZ, QY, QX = DZ // 4, DY // 4, DX // 4
 SLOT = 16
 HALF = DZ // 2
+GROUP = 4
 VMEM_BYTES = 32 * 2**20
 NEIGHBOURS = tuple(o for o in itertools.product((0, 1), (-1, 0, 1), (-1, 0, 1)) if o != (0, 0, 0))
 pair_table = ((0, 0), (1, 1), (2, 2), (0, 1), (0, 2), (1, 2))
@@ -48,6 +49,10 @@
 
 def layer_targets(gz):
     return [0, 4, 8, 12] + ([16, 20] if gz == 0 else [-8, -4])
+
+
+def near_groups(gz):
+    return HALF - GROUP * gz, (DZ - GROUP) * (1 - gz)
 
 
 def constants():
@@ -66,8 +71,9 @@
     near, far = [], []
     for gz in range(2):
         targets = layer_targets(gz)
-        near_z, far_z = HALF * (1 - gz) + np.arange(HALF), HALF * gz + np.arange(HALF)
-        near.append(np.kron(banded(WIDE, R2, near_z, targets).T, ay))
+        far_z = HALF * gz + np.arange(HALF)
+        for z0 in near_groups(gz):
+            near.append(np.kron(banded(WIDE, R2, z0 + np.arange(GROUP), targets).T, ay))
         far.append(np.kron(banded(WIDE, R2, far_z, targets[:QZ]).T, ay))
     mx = np.zeros((DX, 128), np.float32)
     mx[:, :QX] = banded(WIDE, R2, x_all, x_coarse)
@@ -136,8 +142,8 @@
     n_row, n_col, places,
     vol, table,
     out,
-    f, strips, strips_z, send_z, zs, zd, planes, grads, prods, acc, panel, xpanel, zpanel, gpanel, psend, precv,
-    ty, xp, near, far, mx, wpl, wpr, wz, ay, wzx,
+    f, strips, strips_z, send_z, zs_all, zd_all, planes_all, grads_all, prods, acc, xpanel, zpanel, gpanel, psend, precv,
+    ty, xp, near_a, near_b, far, mx, wpl, wpr, wz, ay, wzx,
     local_sem, send_sem, recv_sem,
 ):
     gz, row, col = lax.axis_index("gz"), lax.axis_index("row"), lax.axis_index("col")
@@ -173,7 +179,7 @@
     edge = jnp.where(row == 0, 0, jnp.where(row == n_row - 1, 2, 1))
     fetches = []
     for name, variant, target in (
-        ("ty", edge, ty), ("xp", 0, xp), ("near", gz, near), ("far", gz, far), ("mx", 0, mx),
+        ("ty", edge, ty), ("xp", 0, xp), ("near", 2 * gz, near_a), ("near", 2 * gz + 1, near_b), ("far", gz, far), ("mx", 0, mx),
         ("wp", (col == 0).astype(jnp.int32), wpl), ("wp", 2 + (col == n_col - 1).astype(jnp.int32), wpr),
         ("wz", gz, wz), ("ay", 0, ay), ("wzx", gz, wzx),
     ):
@@ -185,9 +191,42 @@
                     table.at[pl.ds(start, rows)], target.at[:, pl.ds(256 * i, 256)], local_sem.at[1 + len(fetches)]
                 )
             )
+
+    near_z = 13 * (1 - gz)
+    messages, raw, packed = [], [], []
+
+    def message(o, source, target, group):
+        i = len(messages)
+        c = pltpu.make_async_remote_copy(
+            src_ref=source, dst_ref=target, send_sem=send_sem.at[i], recv_sem=recv_sem.at[i],
+            device_id=peer(o), device_id_type=MESH,
+        )
+        messages.append((o, c))
+        group.append((o, c))
+
+    near_layers, halo_layers = pl.ds(near_z, R), pl.ds((R + DZ) * gz, R)
+    both = pl.ds(0, 2)
+    own_kinds = pl.ds(1, 2)
+    y_cut = {0: (pl.ds(0, DY), own_y), 1: (pl.ds(DY - 16, 16), top_y), -1: (pl.ds(0, 16), bottom_y)}
+    for o in sorted(NEIGHBOURS, key=lambda o: -(2 * o[0] + abs(o[1]) + abs(o[2])) - 9 * (o == (1, 0, 0))):
+        a, b, c = o
+        src_y, dst_y = y_cut[b]
+        strip_y = pl.ds(16 + (DY - 16 if b == 1 else 0), DY if b == 0 else 16)
+        if c == 0 and a == 0:
+            message(o, vol.at[:, src_y], f.at[own_z, dst_y], raw)
+            message(o, strips.at[own_kinds, strip_y], strips.at[own_kinds, dst_y], packed)
+        elif c == 0:
+            message(o, vol.at[near_layers, src_y], f.at[halo_layers, dst_y], raw)
+            message(o, send_z.at[both, src_y], strips_z.at[own_kinds, dst_y], packed)
+        else:
+            mine, theirs = (2, 0) if c == 1 else (1, 3)
+            if a == 0:
+                message(o, strips.at[mine, strip_y], strips.at[theirs, dst_y], packed)
+            else:
+                message(o, send_z.at[mine - 1, src_y], strips_z.at[theirs, dst_y], packed)
+
     for c in fetches:
         c.start()
-
     dead_z = pl.ds((R + DZ) * gz, R)
     f[dead_z] = jnp.zeros((R, WY, DX), jnp.bfloat16)
     for d, where_y in ((-1, top_y), (1, bottom_y)):
@@ -203,7 +242,6 @@
             strips_z[kind] = jnp.zeros((WY, 128), jnp.bfloat16)
 
     load.wait()
-    near_z = 13 * (1 - gz)
 
     def pack(layers):
         lane = lax.broadcasted_iota(jnp.int32, (DY, 128), 1)
@@ -223,121 +261,122 @@
     send_z[0] = first
     send_z[1] = last
 
-    messages = []
-
-    def message(o, source, target):
-        i = len(messages)
-        c = pltpu.make_async_remote_copy(
-            src_ref=source, dst_ref=target, send_sem=send_sem.at[i], recv_sem=recv_sem.at[i],
-            device_id=peer(o), device_id_type=MESH,
-        )
-        messages.append((o, c))
-
-    near_layers, halo_layers = pl.ds(near_z, R), pl.ds((R + DZ) * gz, R)
-    both = pl.ds(0, 2)
-    own_kinds = pl.ds(1, 2)
-    y_cut = {0: (pl.ds(0, DY), own_y), 1: (pl.ds(DY - 16, 16), top_y), -1: (pl.ds(0, 16), bottom_y)}
-    for o in sorted(NEIGHBOURS, key=lambda o: -(2 * o[0] + abs(o[1]) + abs(o[2])) - 9 * (o == (1, 0, 0))):
-        a, b, c = o
-        src_y, dst_y = y_cut[b]
-        strip_y = pl.ds(16 + (DY - 16 if b == 1 else 0), DY if b == 0 else 16)
-        if c == 0 and a == 0:
-            message(o, vol.at[:, src_y], f.at[own_z, dst_y])
-            message(o, strips.at[own_kinds, strip_y], strips.at[own_kinds, dst_y])
-        elif c == 0:
-            message(o, vol.at[near_layers, src_y], f.at[halo_layers, dst_y])
-            message(o, send_z.at[both, src_y], strips_z.at[own_kinds, dst_y])
-        else:
-            mine, theirs = (2, 0) if c == 1 else (1, 3)
-            if a == 0:
-                message(o, strips.at[mine, strip_y], strips.at[theirs, dst_y])
-            else:
-                message(o, send_z.at[mine - 1, src_y], strips_z.at[theirs, dst_y])
-
     pl.semaphore_wait(barrier, count)
-    for o, c in messages:
+    for o, c in raw:
+        when(o, lambda c=c: c.start())
+    for o, c in packed:
         when(o, lambda c=c: c.start())
     for c in fetches:
         c.wait()
-    for o, c in messages:
-        when((o[0], -o[1], -o[2]), lambda c=c: c.wait_recv())
+
+    def arrive(group):
+        for o, c in group:
+            when((o[0], -o[1], -o[2]), lambda c=c: c.wait_recv())
 
     def products(get, put):
         g = [get(i) for i in range(3)]
         for c, (i, j) in enumerate(pair_table):
             put(c, g[i] * g[j])
 
-    for side, (k, w) in enumerate(((0, wpl), (2, wpr))):
-        for t in range(3):
-            src = [(strips[i, :, 128 * t : 128 * t + 128] if t < 2 else strips_z[i]) for i in (k, k + 1)]
-            xs = mm(jnp.concatenate(src, axis=1), w[...]).astype(jnp.bfloat16)
-            xpanel[0, :, 128 * t : 128 * t + 128] = xs[:, :128]
-            xpanel[1, :, 128 * t : 128 * t + 128] = xs[:, 128:]
+    def panel_stages():
+        for side, (k, w) in enumerate(((0, wpl), (2, wpr))):
+            rows = []
+            for t in range(3):
+                src = [(strips[i, :, 128 * t : 128 * t + 128] if t < 2 else strips_z[i]) for i in (k, k + 1)]
+                rows.append(jnp.concatenate(src, axis=1))
+            xs = mm(jnp.concatenate(rows, axis=0), w[...]).astype(jnp.bfloat16)
+            for t in range(3):
+                part = xs[WY * t : WY * t + WY]
+                xpanel[0, WY * side : WY * side + WY, 128 * t : 128 * t + 128] = part[:, :128]
+                xpanel[1, WY * side : WY * side + WY, 128 * t : 128 * t + 128] = part[:, 128:]
+        yield
+        both_z = mm(xpanel[0], wz[...]).astype(jnp.bfloat16)
         zpanel[0] = mm(xpanel[1], wz[:, :256]).astype(jnp.bfloat16)
-        zpanel[1] = mm(xpanel[0], wz[:, :256]).astype(jnp.bfloat16)
-        zpanel[2] = mm(xpanel[0], wz[:, 256:]).astype(jnp.bfloat16)
+        zpanel[1] = both_z[:, :256]
+        zpanel[2] = both_z[:, 256:]
+        yield
         edge_grads = [
-            mm(ty[:GY, :WY] if i != 1 else ty[GY:, :WY], zpanel[i]).astype(jnp.bfloat16) for i in range(3)
+            [
+                mm(ty[:GY, :WY] if i != 1 else ty[GY:, :WY], zpanel[i, WY * side : WY * side + WY]).astype(jnp.bfloat16)
+                for i in range(3)
+            ]
+            for side in range(2)
         ]
-
-        def put(c, p, side=side):
-            gpanel[16 * c : 16 * c + 16, 256 * side : 256 * side + 256] = mm(ay[:, :GY], p).astype(jnp.bfloat16)
-
-        products(lambda i: edge_grads[i], put)
-    panel[...] = mm(gpanel[...], wzx[...])
-
-    def gradients(z_base):
-        def four_layers(g, _):
-            z0 = z_base + 4 * g
-            for y in range(0, WY, 16):
-                for x in range(0, DX, 128):
-                    v = [f[z0 + i, y : y + 16, x : x + 128].astype(F32) for i in range(4 + 2 * R)]
-                    for j in range(4):
-                        c = v[j : j + 7]
-                        smooth, slope = c[3] * float(SMOOTH[R]), None
-                        for s in (1, 2, 3):
-                            smooth = smooth + (c[3 - s] + c[3 + s]) * float(SMOOTH[R + s])
-                            term = (c[3 + s] - c[3 - s]) * float(SLOPE[R + s])
-                            slope = term if slope is None else slope + term
-                        zs[j, y : y + 16, x : x + 128] = smooth.astype(jnp.bfloat16)
-                        zd[j, y : y + 16, x : x + 128] = slope.astype(jnp.bfloat16)
-            for j in range(4):
-                pair = mm(ty[:, :WY], zs[j]).astype(jnp.bfloat16)
-                at = slice(GY * j, GY * j + GY)
-                planes[0, at] = pair[:GY]
-                planes[1, at] = pair[GY:]
-                planes[2, at] = mm(ty[:GY, :WY], zd[j]).astype(jnp.bfloat16)
-            for i in range(3):
-                grads[i] = mm(planes[i], xp[:DX] if i == 0 else xp[DX:]).astype(jnp.bfloat16)
-            for y in range(0, 4 * GY, 16):
-                at = pl.ds(pl.multiple_of(4 * GY * g, 16) + y, 16)
-
-                def put(c, p, at=at):
-                    prods[c, at] = p
-
-                products(lambda i, y=y: grads[i, y : y + 16], put)
-            return 0
-
-        lax.fori_loop(0, 2, four_layers, 0)
-
-    gradients(HALF * (1 - gz))
+        yield
+        for side in range(2):
+
+            def put(c, p, side=side):
+                gpanel[16 * c : 16 * c + 16, 256 * side : 256 * side + 256] = mm(ay[:, :GY], p).astype(jnp.bfloat16)
+
+            products(lambda i, side=side: edge_grads[side][i], put)
+        yield
+
+    def layer_stages(z0, g):
+        zs, zd, planes, grads = zs_all.at[g], zd_all.at[g], planes_all.at[g], grads_all.at[g]
+        for y in range(0, WY, 16):
+            for x in range(0, DX, 128):
+                v = [f[z0 + i, y : y + 16, x : x + 128].astype(F32) for i in range(GROUP + 2 * R)]
+                for j in range(GROUP):
+                    c = v[j : j + 7]
+                    smooth, slope = c[3] * float(SMOOTH[R]), None
+                    for s in (1, 2, 3):
+                        smooth = smooth + (c[3 - s] + c[3 + s]) * float(SMOOTH[R + s])
+                        term = (c[3 + s] - c[3 - s]) * float(SLOPE[R + s])
+                        slope = term if slope is None else slope + term
+                    zs[j, y : y + 16, x : x + 128] = smooth.astype(jnp.bfloat16)
+                    zd[j, y : y + 16, x : x + 128] = slope.astype(jnp.bfloat16)
+        yield
+        for j in range(GROUP):
+            pair = mm(ty[:, :WY], zs[j]).astype(jnp.bfloat16)
+            at = slice(GY * j, GY * j + GY)
+            planes[0, at] = pair[:GY]
+            planes[1, at] = pair[GY:]
+            planes[2, at] = mm(ty[:GY, :WY], zd[j]).astype(jnp.bfloat16)
+        yield
+        for i in range(3):
+            grads[i] = mm(planes[i], xp[:DX] if i == 0 else xp[DX:]).astype(jnp.bfloat16)
+        yield
+        for y in range(0, GROUP * GY, 16):
+
+            def put(c, p, y=y):
+                prods[c, GROUP * GY * g + y : GROUP * GY * g + y + 16] = p
+
+            products(lambda i, y=y: grads[i, y : y + 16], put)
+        yield
+
+    def interleave(*stages):
+        for _ in zip(*stages):
+            pass
+
+    part = GROUP * GY
+    rows_first = [(o, c) for o, c in raw if o[0] == 0]
+    arrive(rows_first)
+    interleave(layer_stages(HALF - GROUP * gz, 0))
     for c in range(6):
-        s = mm(near[:, : HALF * GY], prods[c])
-        acc[c] = s[: QZ * QY]
+        acc[c] = mm(near_a[:, :part], prods[c, :part])
+
+    arrive([(o, c) for o, c in raw if o[0] == 1] + packed)
+    interleave(panel_stages(), layer_stages((DZ - GROUP) * (1 - gz), 1))
+    edge_part = mm(gpanel[...], wzx[:, 128 * QZ :])
+    for c in range(6):
+        s = acc[c] + mm(near_b[:, :part], prods[c, part:])
+        acc[c, : QZ * QY] = s[: QZ * QY]
         reach = mm(s[QZ * QY :].astype(jnp.bfloat16), mx[:, :128])
         for q in range(2):
-            edge_part = panel[16 * c : 16 * c + 16, 128 * (QZ + q) : 128 * (QZ + q) + 128]
-            psend[c, 16 * q : 16 * q + 16] = (reach[16 * q : 16 * q + 16] + edge_part).astype(jnp.bfloat16)
-    message((1, 0, 0), psend, precv)
+            edge_q = edge_part[16 * c : 16 * c + 16, 128 * q : 128 * q + 128]
+            psend[c, 16 * q : 16 * q + 16] = (reach[16 * q : 16 * q + 16] + edge_q).astype(jnp.bfloat16)
+    message((1, 0, 0), psend, precv, [])
     messages[-1][1].start()
 
-    gradients(HALF * gz)
+    interleave(layer_stages(HALF * gz, 0))
+    interleave(layer_stages(HALF * gz + GROUP, 1))
+    edge_part = mm(gpanel[...], wzx[:, : 128 * QZ])
     for c in range(6):
-        s = acc[c] + mm(far[:, : HALF * GY], prods[c])
+        s = acc[c, : QZ * QY] + mm(far[:, : 2 * part], prods[c])
         own = mm(s.astype(jnp.bfloat16), mx[:, :128])
         for q in range(QZ):
-            part = own[16 * q : 16 * q + 16] + panel[16 * c : 16 * c + 16, 128 * q : 128 * q + 128]
-            out[c, q] = part[:, :QX]
+            whole = own[16 * q : 16 * q + 16] + edge_part[16 * c : 16 * c + 16, 128 * q : 128 * q + 128]
+            out[c, q] = whole[:, :QX]
     messages[-1][1].wait_recv()
     for q in range(2):
         for c in range(6):
@@ -365,21 +404,21 @@
                 pltpu.VMEM((4, WY, 256), bf),
                 pltpu.VMEM((4, WY, 128), bf),
                 pltpu.VMEM((2, DY, 128), bf),
-                pltpu.VMEM((4, WY, DX), bf),
-                pltpu.VMEM((4, WY, DX), bf),
-                pltpu.VMEM((3, 4 * GY, DX), bf),
-                pltpu.VMEM((3, 4 * GY, DX), bf),
+                pltpu.VMEM((2, 4, WY, DX), bf),
+                pltpu.VMEM((2, 4, WY, DX), bf),
+                pltpu.VMEM((2, 3, 4 * GY, DX), bf),
+                pltpu.VMEM((2, 3, 4 * GY, DX), bf),
                 pltpu.VMEM((6, HALF * GY, DX), bf),
-                pltpu.VMEM((6, QZ * QY, DX), F32),
-                pltpu.VMEM((96, 768), F32),
-                pltpu.VMEM((2, WY, 384), bf),
-                pltpu.VMEM((3, WY, 256), bf),
+                pltpu.VMEM((6, (QZ + 2) * QY, DX), F32),
+                pltpu.VMEM((2, 2 * WY, 384), bf),
+                pltpu.VMEM((3, 2 * WY, 256), bf),
                 pltpu.VMEM((96, 512), bf),
                 pltpu.VMEM((6, 32, 128), bf),
                 pltpu.VMEM((6, 32, 128), bf),
                 pltpu.VMEM((2 * GY, 256), bf),
                 pltpu.VMEM((2 * DX, DX), bf),
-                pltpu.VMEM((6 * 16, 768), bf),
+                pltpu.VMEM((6 * 16, 512), bf),
+                pltpu.VMEM((6 * 16, 512), bf),
                 pltpu.VMEM((4 * 16, 768), bf),
                 pltpu.VMEM((DX, 256), bf),
                 pltpu.VMEM((256, 256), bf),

time: 23.1 us -> 20.8 us (0.900)
  the two profiles are of different devices: /device:TPU:1 before, /device:TPU:96 now
where the time goes in v2:
time: 20.8 us
  Pallas kernels  20.1 us (97%)
  local copies, waits for them, and re-layouts  0.68 us (3%)
    pallas_call x1, Pallas kernels, per_device(): pl.pallas_call(lambda *refs: kernel(n_row, n_col, places, *refs), name='s...  20.1 us
    unnamed x1, local copies, waits for them, and re-layouts  0.68 us

profile of v2, /device:TPU:96, one launch (start us, length us, event | category | flops | bytes accessed | tf_op | source)
XLA Modules:
  0.0 20.8 jit_solution(6870881877358169263)
XLA Ops:
  0.0 20.1 %structure_tensor.1 = f32[6,4,16,64]{3,2,1,0:T(8,128)S(1)} custom-call(bf16[16,64,256]{2,1,0:T(8,128)(2,1)} %refs_0_.1, bf16[8048,256]{1,0:T(8,128)(2,1)} %constant.2.clone.refs_1_), custom_call_target="tpu_custom_call" | custom-call | tf_op jit(solution)/shard_map/structure_tensor/pallas_call | solution.py:396
  20.1 0.7 %copy.4 = f32[6,4,16,64]{3,2,1,0:T(8,128)} copy(f32[6,4,16,64]{3,2,1,0:T(8,128)S(1)} %structure_tensor.1) | data formatting | bytes 196608

commit v3 on v2

--- a/solution.py
+++ b/solution.py
@@ -75,10 +75,10 @@
         for z0 in near_groups(gz):
             near.append(np.kron(banded(WIDE, R2, z0 + np.arange(GROUP), targets).T, ay))
         far.append(np.kron(banded(WIDE, R2, far_z, targets[:QZ]).T, ay))
-    mx = np.zeros((DX, 128), np.float32)
-    mx[:, :QX] = banded(WIDE, R2, x_all, x_coarse)
-    mx[:R] = 0
-    mx[DX - R :] = 0
+    mx = np.zeros((2, DX, 2, QX), np.float32)
+    for i in range(2):
+        mx[i, R : DX - R, i] = banded(WIDE, R2, x_all[R : DX - R], x_coarse)
+    mx = mx.reshape(2 * DX, 2 * QX)
     cols = np.arange(MARGIN)
     pad_in, pad_out = ((0, SLOT - MARGIN), (0, SLOT - MARGIN)), ((0, 0), (0, 0))
     wp = []
@@ -114,7 +114,7 @@
         sides = []
         for x_out in (cols - R2, cols + DX - R):
             bx = np.zeros((SLOT, 128), np.float32)
-            bx[:MARGIN, :QX] = banded(WIDE, R2, x_out, x_coarse)
+            bx[:MARGIN] = np.tile(banded(WIDE, R2, x_out, x_coarse), 2)
             sides.append(np.kron(bz, bx))
         wzx.append(np.concatenate(sides, axis=0))
     named = {"ty": ty, "xp": [x_pair.reshape(2 * DX, DX)], "near": near, "far": far, "mx": [mx], "wp": wp, "wz": wz, "ay": [ay], "wzx": wzx}
@@ -142,7 +142,7 @@
     n_row, n_col, places,
     vol, table,
     out,
-    f, strips, strips_z, send_z, zs_all, zd_all, planes_all, grads_all, prods, acc, xpanel, zpanel, gpanel, psend, precv,
+    f, strips, strips_z, send_z, fold_send, fold_recv, zs_all, zd_all, planes_all, grads_all, prods, acc, xpanel, zpanel, gpanel, psend, precv,
     ty, xp, near_a, near_b, far, mx, wpl, wpr, wz, ay, wzx,
     local_sem, send_sem, recv_sem,
 ):
@@ -205,7 +205,6 @@
         group.append((o, c))
 
     near_layers, halo_layers = pl.ds(near_z, R), pl.ds((R + DZ) * gz, R)
-    both = pl.ds(0, 2)
     own_kinds = pl.ds(1, 2)
     y_cut = {0: (pl.ds(0, DY), own_y), 1: (pl.ds(DY - 16, 16), top_y), -1: (pl.ds(0, 16), bottom_y)}
     for o in sorted(NEIGHBOURS, key=lambda o: -(2 * o[0] + abs(o[1]) + abs(o[2])) - 9 * (o == (1, 0, 0))):
@@ -217,11 +216,12 @@
             message(o, strips.at[own_kinds, strip_y], strips.at[own_kinds, dst_y], packed)
         elif c == 0:
             message(o, vol.at[near_layers, src_y], f.at[halo_layers, dst_y], raw)
-            message(o, send_z.at[both, src_y], strips_z.at[own_kinds, dst_y], packed)
         else:
             mine, theirs = (2, 0) if c == 1 else (1, 3)
             if a == 0:
                 message(o, strips.at[mine, strip_y], strips.at[theirs, dst_y], packed)
+            elif b == 0:
+                message(o, fold_send.at[mine - 1], fold_recv.at[theirs // 2], packed)
             else:
                 message(o, send_z.at[mine - 1, src_y], strips_z.at[theirs, dst_y], packed)
 
@@ -234,37 +234,38 @@
         def _(where_y=where_y):
             f[:, where_y] = jnp.zeros((DZ + 2 * R, 16, DX), jnp.bfloat16)
             strips[:, where_y] = jnp.zeros((4, 16, 256), jnp.bfloat16)
-            strips_z[:, where_y] = jnp.zeros((4, 16, 128), jnp.bfloat16)
+            for kind in (0, 3):
+                strips_z[kind, where_y] = jnp.zeros((16, 128), jnp.bfloat16)
     for d, kind in ((-1, 0), (1, 3)):
         @pl.when(jnp.logical_not(has[2, d]))
         def _(kind=kind):
             strips[kind] = jnp.zeros((WY, 256), jnp.bfloat16)
             strips_z[kind] = jnp.zeros((WY, 128), jnp.bfloat16)
+            fold_recv[kind // 2] = jnp.zeros((DY // 2, 128), jnp.bfloat16)
 
     load.wait()
 
-    def pack(layers):
-        lane = lax.broadcasted_iota(jnp.int32, (DY, 128), 1)
-        first, last = (jnp.zeros((DY, 128), F32) for _ in range(2))
+    def pack(layers, y=16, rows=DY):
+        lane = lax.broadcasted_iota(jnp.int32, (rows, 128), 1)
+        first, last = (jnp.zeros((rows, 128), F32) for _ in range(2))
         for t, z in enumerate(layers):
-            tile = f[R + z, 16 : 16 + DY, :]
+            tile = f[z, y : y + rows, :]
             use = (lane >= SLOT * t) & (lane < SLOT * t + MARGIN)
             first = jnp.where(use, pltpu.roll(tile[:, :128].astype(F32), SLOT * t, 1), first)
             last = jnp.where(use, pltpu.roll(tile[:, 128:].astype(F32), (SLOT * t + MARGIN) % 128, 1), last)
         return first.astype(jnp.bfloat16), last.astype(jnp.bfloat16)
 
     for h in range(2):
-        first, last = pack([HALF * h + t for t in range(8)])
+        first, last = pack([R + HALF * h + t for t in range(8)])
         strips[1, 16 : 16 + DY, 128 * h : 128 * h + 128] = first
         strips[2, 16 : 16 + DY, 128 * h : 128 * h + 128] = last
-    first, last = pack([near_z + t for t in range(R)])
-    send_z[0] = first
-    send_z[1] = last
+    for i, packed_z in enumerate(pack([R + near_z + t for t in range(R)])):
+        send_z[i] = packed_z
+        lower = pltpu.roll(packed_z[DY // 2 :].astype(F32), 64, 1)
+        fold_send[i] = (packed_z[: DY // 2].astype(F32) + lower).astype(jnp.bfloat16)
 
     pl.semaphore_wait(barrier, count)
-    for o, c in raw:
-        when(o, lambda c=c: c.start())
-    for o, c in packed:
+    for o, c in packed + raw:
         when(o, lambda c=c: c.start())
     for c in fetches:
         c.wait()
@@ -279,6 +280,11 @@
             put(c, g[i] * g[j])
 
     def panel_stages():
+        halo_z = (R + DZ) * (1 - gz)
+        for i, packed_z in enumerate(pack([halo_z + t for t in range(R)], 0, WY)):
+            strips_z[1 + i] = packed_z
+            strips_z[3 * i, 16 : 16 + DY // 2] = fold_recv[i]
+            strips_z[3 * i, 16 + DY // 2 : 16 + DY] = pltpu.roll(fold_recv[i].astype(F32), 64, 1).astype(jnp.bfloat16)
         for side, (k, w) in enumerate(((0, wpl), (2, wpr))):
             rows = []
             for t in range(3):
@@ -358,13 +364,17 @@
     arrive([(o, c) for o, c in raw if o[0] == 1] + packed)
     interleave(panel_stages(), layer_stages((DZ - GROUP) * (1 - gz), 1))
     edge_part = mm(gpanel[...], wzx[:, 128 * QZ :])
-    for c in range(6):
-        s = acc[c] + mm(near_b[:, :part], prods[c, part:])
-        acc[c, : QZ * QY] = s[: QZ * QY]
-        reach = mm(s[QZ * QY :].astype(jnp.bfloat16), mx[:, :128])
+    low = lax.broadcasted_iota(jnp.int32, (16, 2 * QX), 1) < QX
+    for pair in range(3):
+        reach = []
+        for c in (2 * pair, 2 * pair + 1):
+            s = acc[c] + mm(near_b[:, :part], prods[c, part:])
+            acc[c, : QZ * QY] = s[: QZ * QY]
+            reach.append(s[QZ * QY :].astype(jnp.bfloat16))
+        reach = mm(jnp.concatenate(reach, axis=1), mx[:, :128])
         for q in range(2):
-            edge_q = edge_part[16 * c : 16 * c + 16, 128 * q : 128 * q + 128]
-            psend[c, 16 * q : 16 * q + 16] = (reach[16 * q : 16 * q + 16] + edge_q).astype(jnp.bfloat16)
+            even, odd = (edge_part[16 * c : 16 * c + 16, 128 * q : 128 * q + 128] for c in (2 * pair, 2 * pair + 1))
+            psend[pair, 16 * q : 16 * q + 16] = (reach[16 * q : 16 * q + 16] + jnp.where(low, even, odd)).astype(jnp.bfloat16)
     message((1, 0, 0), psend, precv, [])
     messages[-1][1].start()
 
@@ -373,17 +383,18 @@
     edge_part = mm(gpanel[...], wzx[:, : 128 * QZ])
     for c in range(6):
         s = acc[c, : QZ * QY] + mm(far[:, : 2 * part], prods[c])
-        own = mm(s.astype(jnp.bfloat16), mx[:, :128])
+        own = mm(s.astype(jnp.bfloat16), mx[:DX, :128])
         for q in range(QZ):
             whole = own[16 * q : 16 * q + 16] + edge_part[16 * c : 16 * c + 16, 128 * q : 128 * q + 128]
             out[c, q] = whole[:, :QX]
+    for o, c in messages[:-1]:
+        when(o, lambda c=c: c.wait_send())
     messages[-1][1].wait_recv()
     for q in range(2):
         for c in range(6):
-            got = precv[c, 16 * q : 16 * q + 16, :QX].astype(F32)
+            got = precv[c // 2, 16 * q : 16 * q + 16, QX * (c % 2) : QX * (c % 2) + QX].astype(F32)
             out[c, 2 * (1 - gz) + q] += got
-    for o, c in messages:
-        when(o, lambda c=c: c.wait_send())
+    messages[-1][1].wait_send()
 
 
 def solution(mesh):
@@ -404,6 +415,8 @@
                 pltpu.VMEM((4, WY, 256), bf),
                 pltpu.VMEM((4, WY, 128), bf),
                 pltpu.VMEM((2, DY, 128), bf),
+                pltpu.VMEM((2, DY // 2, 128), bf),
+                pltpu.VMEM((2, DY // 2, 128), bf),
                 pltpu.VMEM((2, 4, WY, DX), bf),
                 pltpu.VMEM((2, 4, WY, DX), bf),
                 pltpu.VMEM((2, 3, 4 * GY, DX), bf),
@@ -413,14 +426,14 @@
                 pltpu.VMEM((2, 2 * WY, 384), bf),
                 pltpu.VMEM((3, 2 * WY, 256), bf),
                 pltpu.VMEM((96, 512), bf),
-                pltpu.VMEM((6, 32, 128), bf),
-                pltpu.VMEM((6, 32, 128), bf),
+                pltpu.VMEM((3, 32, 128), bf),
+                pltpu.VMEM((3, 32, 128), bf),
                 pltpu.VMEM((2 * GY, 256), bf),
                 pltpu.VMEM((2 * DX, DX), bf),
                 pltpu.VMEM((6 * 16, 512), bf),
                 pltpu.VMEM((6 * 16, 512), bf),
                 pltpu.VMEM((4 * 16, 768), bf),
-                pltpu.VMEM((DX, 256), bf),
+                pltpu.VMEM((2 * DX, 256), bf),
                 pltpu.VMEM((256, 256), bf),
                 pltpu.VMEM((256, 256), bf),
                 pltpu.VMEM((384, 512), bf),

time: 20.8 us -> 18.7 us (0.90)
  the two profiles are of different devices: /device:TPU:96 before, /device:TPU:34 now
where the time goes in v3:
time: 18.7 us; the launch traced here: 18.6 us
  Pallas kernels  17.9 us (96%)
  local copies, waits for them, and re-layouts  0.68 us (4%)
    pallas_call x1, Pallas kernels, per_device(): pl.pallas_call(lambda *refs: kernel(n_row, n_col, places, *refs), name='s...  17.9 us
    unnamed x1, local copies, waits for them, and re-layouts  0.68 us

profile of v3, /device:TPU:34, one launch (start us, length us, event | category | flops | bytes accessed | tf_op | source)
XLA Modules:
  0.0 18.6 jit_solution(7365137962724434283)
XLA Ops:
  0.0 17.9 %structure_tensor.1 = f32[6,4,16,64]{3,2,1,0:T(8,128)S(1)} custom-call(bf16[16,64,256]{2,1,0:T(8,128)(2,1)} %refs_0_.1, bf16[8304,256]{1,0:T(8,128)(2,1)} %constant.2.clone.refs_1_), custom_call_target="tpu_custom_call" | custom-call | tf_op jit(solution)/shard_map/structure_tensor/pallas_call | solution.py:407
  17.9 0.7 %copy.4 = f32[6,4,16,64]{3,2,1,0:T(8,128)} copy(f32[6,4,16,64]{3,2,1,0:T(8,128)S(1)} %structure_tensor.1) | data formatting | bytes 196608

commit v4 on v3

--- a/solution.py
+++ b/solution.py
@@ -21,7 +21,9 @@
 QZ, QY, QX = DZ // 4, DY // 4, DX // 4
 SLOT = 16
 HALF = DZ // 2
-GROUP = 4
+GROUPS = (HALF - R, R, HALF // 2, HALF // 2)
+STARTS = (0, HALF - R, HALF, HALF + HALF // 2)
+DEEPEST = max(GROUPS)
 VMEM_BYTES = 32 * 2**20
 NEIGHBOURS = tuple(o for o in itertools.product((0, 1), (-1, 0, 1), (-1, 0, 1)) if o != (0, 0, 0))
 pair_table = ((0, 0), (1, 1), (2, 2), (0, 1), (0, 2), (1, 2))
@@ -52,7 +54,7 @@
 
 
 def near_groups(gz):
-    return HALF - GROUP * gz, (DZ - GROUP) * (1 - gz)
+    return HALF - GROUPS[0] * gz, (DZ - R) * (1 - gz)
 
 
 def constants():
@@ -68,13 +70,14 @@
         ty.append(np.concatenate([banded(t, R, y_in, y_out).T * inside[:, None] for t in (SMOOTH, SLOPE)]))
     x_pair = np.stack([banded(SLOPE, R, x_all, x_all), banded(SMOOTH, R, x_all, x_all)])
     ay = banded(WIDE, R2, y_out, y_coarse).T
-    near, far = [], []
+    near_a, near_b, rest = [], [], []
     for gz in range(2):
         targets = layer_targets(gz)
-        far_z = HALF * gz + np.arange(HALF)
-        for z0 in near_groups(gz):
-            near.append(np.kron(banded(WIDE, R2, z0 + np.arange(GROUP), targets).T, ay))
-        far.append(np.kron(banded(WIDE, R2, far_z, targets[:QZ]).T, ay))
+        a, b = (z0 + np.arange(n) for z0, n in zip(near_groups(gz), GROUPS))
+        near_a.append(np.kron(banded(WIDE, R2, a, targets).T, ay))
+        near_b.append(np.kron(banded(WIDE, R2, b, targets[QZ:]).T, ay))
+        rest_z = np.concatenate([b, HALF * gz + np.arange(HALF)])
+        rest.append(np.kron(banded(WIDE, R2, rest_z, targets[:QZ]).T, ay))
     mx = np.zeros((2, DX, 2, QX), np.float32)
     for i in range(2):
         mx[i, R : DX - R, i] = banded(WIDE, R2, x_all[R : DX - R], x_coarse)
@@ -101,23 +104,25 @@
     one = np.eye(SLOT, dtype=np.float32)
     for gz in range(2):
         z_halo = DZ + np.arange(8) if gz == 0 else np.arange(8) - R
+        halves = [HALF * (1 - gz) + np.arange(HALF), HALF * gz + np.arange(HALF)]
         rows = []
         for z_in, used in ((np.arange(DZ), DZ), (z_halo, R)):
             keep = (np.arange(len(z_in)) < used)[:, None]
             rows.append(
                 np.concatenate(
-                    [np.kron(banded(t, R, z_in, np.arange(DZ)) * keep, one) for t in (SMOOTH, SLOPE)], axis=1
+                    [np.kron(banded(t, R, z_in, z_out) * keep, one) for z_out in halves for t in (SMOOTH, SLOPE)], axis=1
                 )
             )
         wz.append(np.concatenate(rows, axis=0))
-        bz = banded(WIDE, R2, np.arange(DZ), layer_targets(gz))
-        sides = []
-        for x_out in (cols - R2, cols + DX - R):
-            bx = np.zeros((SLOT, 128), np.float32)
-            bx[:MARGIN] = np.tile(banded(WIDE, R2, x_out, x_coarse), 2)
-            sides.append(np.kron(bz, bx))
-        wzx.append(np.concatenate(sides, axis=0))
-    named = {"ty": ty, "xp": [x_pair.reshape(2 * DX, DX)], "near": near, "far": far, "mx": [mx], "wp": wp, "wz": wz, "ay": [ay], "wzx": wzx}
+        parts = []
+        for z_out in halves:
+            bz = banded(WIDE, R2, z_out, layer_targets(gz))
+            for x_out in (cols - R2, cols + DX - R):
+                bx = np.zeros((SLOT, 128), np.float32)
+                bx[:MARGIN] = np.tile(banded(WIDE, R2, x_out, x_coarse), 2)
+                parts.append(np.kron(bz, bx))
+        wzx.append(np.concatenate(parts, axis=0))
+    named = {"ty": ty, "xp": [x_pair.reshape(2 * DX, DX)], "near_a": near_a, "near_b": near_b, "rest": rest, "mx": [mx], "wp": wp, "wz": wz, "ay": [ay], "wzx": wzx}
     return pack_table(named)
 
 
@@ -143,7 +148,7 @@
     vol, table,
     out,
     f, strips, strips_z, send_z, fold_send, fold_recv, zs_all, zd_all, planes_all, grads_all, prods, acc, xpanel, zpanel, gpanel, psend, precv,
-    ty, xp, near_a, near_b, far, mx, wpl, wpr, wz, ay, wzx,
+    ty, xp, near_a, near_b, rest, mx, wpl, wpr, wz, ay, wzx,
     local_sem, send_sem, recv_sem,
 ):
     gz, row, col = lax.axis_index("gz"), lax.axis_index("row"), lax.axis_index("col")
@@ -179,7 +184,7 @@
     edge = jnp.where(row == 0, 0, jnp.where(row == n_row - 1, 2, 1))
     fetches = []
     for name, variant, target in (
-        ("ty", edge, ty), ("xp", 0, xp), ("near", 2 * gz, near_a), ("near", 2 * gz + 1, near_b), ("far", gz, far), ("mx", 0, mx),
+        ("ty", edge, ty), ("xp", 0, xp), ("near_a", gz, near_a), ("near_b", gz, near_b), ("rest", gz, rest), ("mx", 0, mx),
         ("wp", (col == 0).astype(jnp.int32), wpl), ("wp", 2 + (col == n_col - 1).astype(jnp.int32), wpr),
         ("wz", gz, wz), ("ay", 0, ay), ("wzx", gz, wzx),
     ):
@@ -279,31 +284,42 @@
         for c, (i, j) in enumerate(pair_table):
             put(c, g[i] * g[j])
 
-    def panel_stages():
+    panel_sides = ((0, wpl), (2, wpr))
+
+    def panel_x(tiles):
+        for side, (k, w) in enumerate(panel_sides):
+            rows = []
+            for t in tiles:
+                src = [(strips[i, :, 128 * t : 128 * t + 128] if t < 2 else strips_z[i]) for i in (k, k + 1)]
+                rows.append(jnp.concatenate(src, axis=1))
+            xs = mm(jnp.concatenate(rows, axis=0), w[...]).astype(jnp.bfloat16)
+            for i, t in enumerate(tiles):
+                piece = xs[WY * i : WY * i + WY]
+                xpanel[0, WY * side : WY * side + WY, 128 * t : 128 * t + 128] = piece[:, :128]
+                xpanel[1, WY * side : WY * side + WY, 128 * t : 128 * t + 128] = piece[:, 128:]
+
+    def panel_halo():
         halo_z = (R + DZ) * (1 - gz)
         for i, packed_z in enumerate(pack([halo_z + t for t in range(R)], 0, WY)):
             strips_z[1 + i] = packed_z
             strips_z[3 * i, 16 : 16 + DY // 2] = fold_recv[i]
             strips_z[3 * i, 16 + DY // 2 : 16 + DY] = pltpu.roll(fold_recv[i].astype(F32), 64, 1).astype(jnp.bfloat16)
-        for side, (k, w) in enumerate(((0, wpl), (2, wpr))):
-            rows = []
-            for t in range(3):
-                src = [(strips[i, :, 128 * t : 128 * t + 128] if t < 2 else strips_z[i]) for i in (k, k + 1)]
-                rows.append(jnp.concatenate(src, axis=1))
-            xs = mm(jnp.concatenate(rows, axis=0), w[...]).astype(jnp.bfloat16)
-            for t in range(3):
-                part = xs[WY * t : WY * t + WY]
-                xpanel[0, WY * side : WY * side + WY, 128 * t : 128 * t + 128] = part[:, :128]
-                xpanel[1, WY * side : WY * side + WY, 128 * t : 128 * t + 128] = part[:, 128:]
-        yield
-        both_z = mm(xpanel[0], wz[...]).astype(jnp.bfloat16)
-        zpanel[0] = mm(xpanel[1], wz[:, :256]).astype(jnp.bfloat16)
-        zpanel[1] = both_z[:, :256]
-        zpanel[2] = both_z[:, 256:]
+        panel_x((2,))
+
+    def panel_stages(half):
+        if half == 0:
+            panel_halo()
+        yield
+        smooth_slope = mm(xpanel[0], wz[:, 256 * half : 256 * half + 256]).astype(jnp.bfloat16)
+        zpanel[half, 0] = mm(xpanel[1], wz[:, 256 * half : 256 * half + 128]).astype(jnp.bfloat16)
+        zpanel[half, 1] = smooth_slope[:, :128]
+        zpanel[half, 2] = smooth_slope[:, 128:]
         yield
         edge_grads = [
             [
-                mm(ty[:GY, :WY] if i != 1 else ty[GY:, :WY], zpanel[i, WY * side : WY * side + WY]).astype(jnp.bfloat16)
+                mm(ty[:GY, :WY] if i != 1 else ty[GY:, :WY], zpanel[half, i, WY * side : WY * side + WY]).astype(
+                    jnp.bfloat16
+                )
                 for i in range(3)
             ]
             for side in range(2)
@@ -311,18 +327,19 @@
         yield
         for side in range(2):
 
-            def put(c, p, side=side):
-                gpanel[16 * c : 16 * c + 16, 256 * side : 256 * side + 256] = mm(ay[:, :GY], p).astype(jnp.bfloat16)
+            def put(c, p, at=256 * half + 128 * side):
+                gpanel[16 * c : 16 * c + 16, at : at + 128] = mm(ay[:, :GY], p).astype(jnp.bfloat16)
 
             products(lambda i, side=side: edge_grads[side][i], put)
         yield
 
     def layer_stages(z0, g):
-        zs, zd, planes, grads = zs_all.at[g], zd_all.at[g], planes_all.at[g], grads_all.at[g]
+        deep, at_row = GROUPS[g], GY * STARTS[g]
+        zs, zd, planes, grads = (ref.at[g % 2] for ref in (zs_all, zd_all, planes_all, grads_all))
         for y in range(0, WY, 16):
             for x in range(0, DX, 128):
-                v = [f[z0 + i, y : y + 16, x : x + 128].astype(F32) for i in range(GROUP + 2 * R)]
-                for j in range(GROUP):
+                v = [f[z0 + i, y : y + 16, x : x + 128].astype(F32) for i in range(deep + 2 * R)]
+                for j in range(deep):
                     c = v[j : j + 7]
                     smooth, slope = c[3] * float(SMOOTH[R]), None
                     for s in (1, 2, 3):
@@ -332,7 +349,7 @@
                     zs[j, y : y + 16, x : x + 128] = smooth.astype(jnp.bfloat16)
                     zd[j, y : y + 16, x : x + 128] = slope.astype(jnp.bfloat16)
         yield
-        for j in range(GROUP):
+        for j in range(deep):
             pair = mm(ty[:, :WY], zs[j]).astype(jnp.bfloat16)
             at = slice(GY * j, GY * j + GY)
             planes[0, at] = pair[:GY]
@@ -340,12 +357,12 @@
             planes[2, at] = mm(ty[:GY, :WY], zd[j]).astype(jnp.bfloat16)
         yield
         for i in range(3):
-            grads[i] = mm(planes[i], xp[:DX] if i == 0 else xp[DX:]).astype(jnp.bfloat16)
-        yield
-        for y in range(0, GROUP * GY, 16):
+            grads[i, : GY * deep] = mm(planes[i, : GY * deep], xp[:DX] if i == 0 else xp[DX:]).astype(jnp.bfloat16)
+        yield
+        for y in range(0, GY * deep, 16):
 
             def put(c, p, y=y):
-                prods[c, GROUP * GY * g + y : GROUP * GY * g + y + 16] = p
+                prods[c, at_row + y : at_row + y + 16] = p
 
             products(lambda i, y=y: grads[i, y : y + 16], put)
         yield
@@ -354,23 +371,24 @@
         for _ in zip(*stages):
             pass
 
-    part = GROUP * GY
+    near_a_z, near_b_z = near_groups(gz)
+    ka, kb = GY * GROUPS[0], GY * GROUPS[1]
     rows_first = [(o, c) for o, c in raw if o[0] == 0]
-    arrive(rows_first)
-    interleave(layer_stages(HALF - GROUP * gz, 0))
+    arrive(rows_first + [(o, c) for o, c in packed if o[0] == 0])
+    panel_x((0, 1))
+    interleave(layer_stages(near_a_z, 0))
     for c in range(6):
-        acc[c] = mm(near_a[:, :part], prods[c, :part])
-
-    arrive([(o, c) for o, c in raw if o[0] == 1] + packed)
-    interleave(panel_stages(), layer_stages((DZ - GROUP) * (1 - gz), 1))
-    edge_part = mm(gpanel[...], wzx[:, 128 * QZ :])
+        acc[c] = mm(near_a[:, :ka], prods[c, :ka])
+
+    arrive([m for group in (raw, packed) for m in group if m[0][0] == 1])
+    interleave(panel_stages(0), layer_stages(near_b_z, 1))
+    edge_part = mm(gpanel[:, :256], wzx[:256, 128 * QZ :])
     low = lax.broadcasted_iota(jnp.int32, (16, 2 * QX), 1) < QX
     for pair in range(3):
-        reach = []
-        for c in (2 * pair, 2 * pair + 1):
-            s = acc[c] + mm(near_b[:, :part], prods[c, part:])
-            acc[c, : QZ * QY] = s[: QZ * QY]
-            reach.append(s[QZ * QY :].astype(jnp.bfloat16))
+        reach = [
+            (acc[c, QZ * QY :] + mm(near_b[:, :kb], prods[c, ka : ka + kb])).astype(jnp.bfloat16)
+            for c in (2 * pair, 2 * pair + 1)
+        ]
         reach = mm(jnp.concatenate(reach, axis=1), mx[:, :128])
         for q in range(2):
             even, odd = (edge_part[16 * c : 16 * c + 16, 128 * q : 128 * q + 128] for c in (2 * pair, 2 * pair + 1))
@@ -378,11 +396,11 @@
     message((1, 0, 0), psend, precv, [])
     messages[-1][1].start()
 
-    interleave(layer_stages(HALF * gz, 0))
-    interleave(layer_stages(HALF * gz + GROUP, 1))
+    interleave(panel_stages(1), layer_stages(HALF * gz, 2))
+    interleave(layer_stages(HALF * gz + GROUPS[2], 3))
     edge_part = mm(gpanel[...], wzx[:, : 128 * QZ])
     for c in range(6):
-        s = acc[c, : QZ * QY] + mm(far[:, : 2 * part], prods[c])
+        s = acc[c, : QZ * QY] + mm(rest[:, : DZ * GY - ka], prods[c, ka:])
         own = mm(s.astype(jnp.bfloat16), mx[:DX, :128])
         for q in range(QZ):
             whole = own[16 * q : 16 * q + 16] + edge_part[16 * c : 16 * c + 16, 128 * q : 128 * q + 128]
@@ -417,22 +435,22 @@
                 pltpu.VMEM((2, DY, 128), bf),
                 pltpu.VMEM((2, DY // 2, 128), bf),
                 pltpu.VMEM((2, DY // 2, 128), bf),
-                pltpu.VMEM((2, 4, WY, DX), bf),
-                pltpu.VMEM((2, 4, WY, DX), bf),
-                pltpu.VMEM((2, 3, 4 * GY, DX), bf),
-                pltpu.VMEM((2, 3, 4 * GY, DX), bf),
-                pltpu.VMEM((6, HALF * GY, DX), bf),
+                pltpu.VMEM((2, DEEPEST, WY, DX), bf),
+                pltpu.VMEM((2, DEEPEST, WY, DX), bf),
+                pltpu.VMEM((2, 3, DEEPEST * GY, DX), bf),
+                pltpu.VMEM((2, 3, DEEPEST * GY, DX), bf),
+                pltpu.VMEM((6, DZ * GY, DX), bf),
                 pltpu.VMEM((6, (QZ + 2) * QY, DX), F32),
                 pltpu.VMEM((2, 2 * WY, 384), bf),
-                pltpu.VMEM((3, 2 * WY, 256), bf),
+                pltpu.VMEM((2, 3, 2 * WY, 128), bf),
                 pltpu.VMEM((96, 512), bf),
                 pltpu.VMEM((3, 32, 128), bf),
                 pltpu.VMEM((3, 32, 128), bf),
                 pltpu.VMEM((2 * GY, 256), bf),
                 pltpu.VMEM((2 * DX, DX), bf),
                 pltpu.VMEM((6 * 16, 512), bf),
-                pltpu.VMEM((6 * 16, 512), bf),
-                pltpu.VMEM((4 * 16, 768), bf),
+                pltpu.VMEM((2 * 16, 256), bf),
+                pltpu.VMEM((4 * 16, 1024), bf),
                 pltpu.VMEM((2 * DX, 256), bf),
                 pltpu.VMEM((256, 256), bf),
                 pltpu.VMEM((256, 256), bf),

time: 18.7 us -> 18.2 us (0.973)
  Pallas kernels: 17.9 us -> 17.5 us
    pallas_call x1, Pallas kernels: 17.9 us -> 17.5 us  [per_device(): pl.pallas_call(lambda *refs: kernel(n_row, n_col, places, *refs), name='s...]
where the time goes in v4:
time: 18.2 us; the launch traced here: 18.1 us
  Pallas kernels  17.5 us (96%)
  local copies, waits for them, and re-layouts  0.68 us (4%)
    pallas_call x1, Pallas kernels, per_device(): pl.pallas_call(lambda *refs: kernel(n_row, n_col, places, *refs), name='s...  17.5 us
    unnamed x1, local copies, waits for them, and re-layouts  0.68 us

profile of v4, /device:TPU:34, one launch (start us, length us, event | category | flops | bytes accessed | tf_op | source)
XLA Modules:
  0.0 18.1 jit_solution(15131677026605236524)
XLA Ops:
  0.0 17.5 %structure_tensor.1 = f32[6,4,16,64]{3,2,1,0:T(8,128)S(1)} custom-call(bf16[16,64,256]{2,1,0:T(8,128)(2,1)} %refs_0_.1, bf16[8112,256]{1,0:T(8,128)(2,1)} %constant.2.clone.refs_1_), custom_call_target="tpu_custom_call" | custom-call | tf_op jit(solution)/shard_map/structure_tensor/pallas_call | solution.py:425
  17.5 0.7 %copy.4 = f32[6,4,16,64]{3,2,1,0:T(8,128)} copy(f32[6,4,16,64]{3,2,1,0:T(8,128)S(1)} %structure_tensor.1) | data formatting | bytes 196608

commit v5 on v4

--- a/solution.py
+++ b/solution.py
@@ -298,10 +298,15 @@
                 xpanel[0, WY * side : WY * side + WY, 128 * t : 128 * t + 128] = piece[:, :128]
                 xpanel[1, WY * side : WY * side + WY, 128 * t : 128 * t + 128] = piece[:, 128:]
 
+    def pack_halo(y, rows):
+        halo_z = (R + DZ) * (1 - gz)
+        for i, packed_z in enumerate(pack([halo_z + t for t in range(R)], y, rows)):
+            strips_z[1 + i, y : y + rows] = packed_z
+
     def panel_halo():
-        halo_z = (R + DZ) * (1 - gz)
-        for i, packed_z in enumerate(pack([halo_z + t for t in range(R)], 0, WY)):
-            strips_z[1 + i] = packed_z
+        for y in (0, 16 + DY):
+            pack_halo(y, 16)
+        for i in range(2):
             strips_z[3 * i, 16 : 16 + DY // 2] = fold_recv[i]
             strips_z[3 * i, 16 + DY // 2 : 16 + DY] = pltpu.roll(fold_recv[i].astype(F32), 64, 1).astype(jnp.bfloat16)
         panel_x((2,))
@@ -333,10 +338,9 @@
             products(lambda i, side=side: edge_grads[side][i], put)
         yield
 
-    def layer_stages(z0, g):
-        deep, at_row = GROUPS[g], GY * STARTS[g]
-        zs, zd, planes, grads = (ref.at[g % 2] for ref in (zs_all, zd_all, planes_all, grads_all))
-        for y in range(0, WY, 16):
+    def filter_z(z0, g, rows):
+        deep, zs, zd = GROUPS[g], zs_all.at[g % 2], zd_all.at[g % 2]
+        for y in rows:
             for x in range(0, DX, 128):
                 v = [f[z0 + i, y : y + 16, x : x + 128].astype(F32) for i in range(deep + 2 * R)]
                 for j in range(deep):
@@ -348,6 +352,11 @@
                         slope = term if slope is None else slope + term
                     zs[j, y : y + 16, x : x + 128] = smooth.astype(jnp.bfloat16)
                     zd[j, y : y + 16, x : x + 128] = slope.astype(jnp.bfloat16)
+
+    def layer_stages(z0, g, rows=range(0, WY, 16)):
+        deep, at_row = GROUPS[g], GY * STARTS[g]
+        zs, zd, planes, grads = (ref.at[g % 2] for ref in (zs_all, zd_all, planes_all, grads_all))
+        filter_z(z0, g, rows)
         yield
         for j in range(deep):
             pair = mm(ty[:, :WY], zs[j]).astype(jnp.bfloat16)
@@ -380,19 +389,24 @@
     for c in range(6):
         acc[c] = mm(near_a[:, :ka], prods[c, :ka])
 
-    arrive([m for group in (raw, packed) for m in group if m[0][0] == 1])
-    interleave(panel_stages(0), layer_stages(near_b_z, 1))
+    arrive(raw[:1])
+    filter_z(near_b_z, 1, range(16, 16 + DY, 16))
+    pack_halo(16, DY)
+
+    arrive([m for group in (packed, raw[1:]) for m in group if m[0][0] == 1])
+    interleave(panel_stages(0), layer_stages(near_b_z, 1, (0, 16 + DY)))
     edge_part = mm(gpanel[:, :256], wzx[:256, 128 * QZ :])
     low = lax.broadcasted_iota(jnp.int32, (16, 2 * QX), 1) < QX
+    reach = [
+        (acc[c, QZ * QY :] + mm(near_b[:, :kb], prods[c, ka : ka + kb])).astype(jnp.bfloat16) for c in range(6)
+    ]
+    reach = jnp.concatenate([jnp.concatenate(reach[i : i + 2], axis=1) for i in (0, 2, 4)], axis=0)
+    reach = mm(reach, mx[:, :128])
     for pair in range(3):
-        reach = [
-            (acc[c, QZ * QY :] + mm(near_b[:, :kb], prods[c, ka : ka + kb])).astype(jnp.bfloat16)
-            for c in (2 * pair, 2 * pair + 1)
-        ]
-        reach = mm(jnp.concatenate(reach, axis=1), mx[:, :128])
         for q in range(2):
             even, odd = (edge_part[16 * c : 16 * c + 16, 128 * q : 128 * q + 128] for c in (2 * pair, 2 * pair + 1))
-            psend[pair, 16 * q : 16 * q + 16] = (reach[16 * q : 16 * q + 16] + jnp.where(low, even, odd)).astype(jnp.bfloat16)
+            at = 32 * pair + 16 * q
+            psend[pair, 16 * q : 16 * q + 16] = (reach[at : at + 16] + jnp.where(low, even, odd)).astype(jnp.bfloat16)
     message((1, 0, 0), psend, precv, [])
     messages[-1][1].start()
 

time: 18.2 us -> 18 us (0.989)
  Pallas kernels: 17.5 us -> 17.2 us
    pallas_call x1, Pallas kernels: 17.5 us -> 17.2 us  [per_device(): pl.pallas_call(lambda *refs: kernel(n_row, n_col, places, *refs), name='s...]
where the time goes in v5:
time: 18 us; the launch traced here: 17.9 us
  Pallas kernels  17.2 us (96%)
  local copies, waits for them, and re-layouts  0.68 us (4%)
    pallas_call x1, Pallas kernels, per_device(): pl.pallas_call(lambda *refs: kernel(n_row, n_col, places, *refs), name='s...  17.2 us
    unnamed x1, local copies, waits for them, and re-layouts  0.68 us

profile of v5, /device:TPU:34, one launch (start us, length us, event | category | flops | bytes accessed | tf_op | source)
XLA Modules:
  0.0 17.9 jit_solution(6013091621417470301)
XLA Ops:
  0.0 17.2 %structure_tensor.1 = f32[6,4,16,64]{3,2,1,0:T(8,128)S(1)} custom-call(bf16[16,64,256]{2,1,0:T(8,128)(2,1)} %refs_0_.1, bf16[8112,256]{1,0:T(8,128)(2,1)} %constant.2.clone.refs_1_), custom_call_target="tpu_custom_call" | custom-call | tf_op jit(solution)/shard_map/structure_tensor/pallas_call | solution.py:439
  17.2 0.7 %copy.4 = f32[6,4,16,64]{3,2,1,0:T(8,128)} copy(f32[6,4,16,64]{3,2,1,0:T(8,128)S(1)} %structure_tensor.1) | data formatting | bytes 196608

commit v6 on v5

--- a/solution.py
+++ b/solution.py
@@ -147,7 +147,7 @@
     n_row, n_col, places,
     vol, table,
     out,
-    f, strips, strips_z, send_z, fold_send, fold_recv, zs_all, zd_all, planes_all, grads_all, prods, acc, xpanel, zpanel, gpanel, psend, precv,
+    f, strips, strips_z, send_z, fold_send, fold_recv, zs_all, zd_all, planes_all, grads_all, prods, acc, xpanel, zown, zpanel, gpanel, psend, precv,
     ty, xp, near_a, near_b, rest, mx, wpl, wpr, wz, ay, wzx,
     local_sem, send_sem, recv_sem,
 ):
@@ -315,8 +315,13 @@
         if half == 0:
             panel_halo()
         yield
-        smooth_slope = mm(xpanel[0], wz[:, 256 * half : 256 * half + 256]).astype(jnp.bfloat16)
-        zpanel[half, 0] = mm(xpanel[1], wz[:, 256 * half : 256 * half + 128]).astype(jnp.bfloat16)
+        if half == 0:
+            halo_part = [mm(xpanel[i, :, 256:], wz[256:, : 256 - 128 * i]) for i in range(2)]
+            smooth_slope = (zown[:, :256] + halo_part[0]).astype(jnp.bfloat16)
+            zpanel[half, 0] = (zown[:, 256:] + halo_part[1]).astype(jnp.bfloat16)
+        else:
+            smooth_slope = mm(xpanel[0], wz[:, 256:]).astype(jnp.bfloat16)
+            zpanel[half, 0] = mm(xpanel[1], wz[:, 256:384]).astype(jnp.bfloat16)
         zpanel[half, 1] = smooth_slope[:, :128]
         zpanel[half, 2] = smooth_slope[:, 128:]
         yield
@@ -385,6 +390,8 @@
     rows_first = [(o, c) for o, c in raw if o[0] == 0]
     arrive(rows_first + [(o, c) for o, c in packed if o[0] == 0])
     panel_x((0, 1))
+    for i in range(2):
+        zown[:, 256 * i : 256 + 128 * i] = mm(xpanel[i, :, :256], wz[:256, : 256 - 128 * i])
     interleave(layer_stages(near_a_z, 0))
     for c in range(6):
         acc[c] = mm(near_a[:, :ka], prods[c, :ka])
@@ -456,6 +463,7 @@
                 pltpu.VMEM((6, DZ * GY, DX), bf),
                 pltpu.VMEM((6, (QZ + 2) * QY, DX), F32),
                 pltpu.VMEM((2, 2 * WY, 384), bf),
+                pltpu.VMEM((2 * WY, 384), F32),
                 pltpu.VMEM((2, 3, 2 * WY, 128), bf),
                 pltpu.VMEM((96, 512), bf),
                 pltpu.VMEM((3, 32, 128), bf),

time: 18 us -> 18 us (level)
  no operation moved by 1% of the time
where the time goes in v6:
time: 18 us; the launch traced here: 17.9 us
  Pallas kernels  17.2 us (96%)
  local copies, waits for them, and re-layouts  0.68 us (4%)
    pallas_call x1, Pallas kernels, per_device(): pl.pallas_call(lambda *refs: kernel(n_row, n_col, places, *refs), name='s...  17.2 us
    unnamed x1, local copies, waits for them, and re-layouts  0.68 us

profile of v6, /device:TPU:34, one launch (start us, length us, event | category | flops | bytes accessed | tf_op | source)
XLA Modules:
  0.0 17.9 jit_solution(13131349440679016518)
XLA Ops:
  0.0 17.2 %structure_tensor.1 = f32[6,4,16,64]{3,2,1,0:T(8,128)S(1)} custom-call(bf16[16,64,256]{2,1,0:T(8,128)(2,1)} %refs_0_.1, bf16[8112,256]{1,0:T(8,128)(2,1)} %constant.2.clone.refs_1_), custom_call_target="tpu_custom_call" | custom-call | tf_op jit(solution)/shard_map/structure_tensor/pallas_call | solution.py:446
  17.2 0.7 %copy.4 = f32[6,4,16,64]{3,2,1,0:T(8,128)} copy(f32[6,4,16,64]{3,2,1,0:T(8,128)S(1)} %structure_tensor.1) | data formatting | bytes 196608
